TPU v7x, 256 devices: a whole 4x4x8 slice. The times are simulated.
256 devices in a mesh: sec: 64 (over z, x, core), cell: 4 (over y).
Axes of the slice: x: 4, y: 4, z: 8, core: 2. Of those that a mesh axis runs over, the one named last changes fastest.
Arguments:
- fluid_delta: float32 [7, 8, 131072], P(None, None, ('sec', 'cell')), may hold values from -6 to 6
- jacobian: bfloat16 [7, 8, 8, 131072], P(None, None, None, ('sec', 'cell')), may hold values from -0.75 to 0.75
- face_nbr: int32 [6, 131072], P(None, ('sec', 'cell')), may hold values from -128 to 128, as said below
- freq_col: float32 [7, 8, 131072], P(None, None, ('sec', 'cell')), may hold values from -6 to 6
- grid_sens: float32 [8, 3, 131072], P(None, None, ('sec', 'cell')), may hold values from -0.15625 to 0.15625
- cell_xyz: float32 [3, 131072], P(None, ('sec', 'cell')), may hold values from 0 to 1
- surf_cell: int32 [65536], P(('sec', 'cell')), may hold values from 0 to 511
- surf_owner: int32 [65536, 1], P(('sec', 'cell')), may hold values from 0 to 63; in each aligned block of 256 rows (0 to 255, 256 to 511, ...) at most 16 rows name the same one
- surf_node: int32 [65536], P(('sec', 'cell')), may hold values from 0 to 127
- load_proj: float32 [3, 8, 65536], P(None, None, ('sec', 'cell')), may hold values from -2 to 2
- surf_xyz: float32 [3, 65536], P(None, ('sec', 'cell')), may hold values from 0 to 1
- struct_delta: float32 [7, 3, 32768], P(None, None, ('sec', 'cell')), may hold values from -6 to 6
- stiffness: float32 [3, 128, 3, 32768], P(None, None, None, ('sec', 'cell')), may hold values from -0.3125 to 0.3125
- mass: float32 [3, 32768], P(None, ('sec', 'cell')), may hold values from 0.2 to 1
- omega: float32 [1], replicated, may hold values from 0.6 to 1.6
- freq_delta: float32 [1], replicated, may hold values from -4 to 4
- phase_row: float32 [7, 8, 131072], P(None, None, ('sec', 'cell')), may hold values from -0.0066439068 to 0.0066439068
Outputs:
- fluid_out: float32 [7, 8, 131072], P(None, None, ('sec', 'cell'))
- struct_out: float32 [7, 3, 32768], P(None, None, ('sec', 'cell'))
- phase_out: float32 [1], replicated
Inputs may be any that keep to these rules, and one draw needn't show every extreme that they name: `face_nbr`: every nonzero offset leads to a cell of the grid; both distances 128 occur. `surf_owner`: the surface rows of one aligned block of 256 rows name one owner at most 16 times.
All inputs are finite; a program needn't handle non-finite values.
Results may differ from a plain program's by a relative error of at most 0.0003.
Values sent between devices are 32-bit elements; how exact they have to be, the bound alone decides.
No kernel may reach another device: no remote copies, remote signals or barrier semaphores. Data moves between devices by JAX's collectives and lax.ppermute only.
A program may use at most 128 MiB of HBM per device.

v0:
```python
import functools

import jax
import jax.numpy as jnp
import numpy as np
from jax import lax
from jax.experimental import pallas as pl
from jax.experimental.pallas import tpu as pltpu
from jax.sharding import PartitionSpec as P

NT = 7
NV = 8
NF = 6
L = 128
CHIPS = 32
CAP = 16
ROWS = 27
F32 = jnp.float32
BF16 = jnp.bfloat16


def spectral_table(instances):
    positions = np.arange(instances)
    offset = positions[:, None] - positions[None, :]
    clipped = np.where(offset == 0, 1, offset)
    return np.where(
        offset == 0, 0.0, 0.5 * (-1.0) ** offset / np.sin(np.pi * clipped / instances)
    )


SPECTRAL = np.asarray(spectral_table(NT), np.float32)
SECOND = np.asarray(spectral_table(NT) @ spectral_table(NT), np.float32)


def iota(shape, axis):
    return lax.broadcasted_iota(jnp.int32, shape, axis)


def lanes_of(values, index):
    return jnp.take_along_axis(values, index, axis=1, mode="promise_in_bounds")


def thirds(values):
    high = values.astype(BF16)
    rest = values - high.astype(F32)
    middle = rest.astype(BF16)
    low = (rest - middle.astype(F32)).astype(BF16)
    return jnp.concatenate([high, middle, low], axis=0)


def dot_nt(a, b, precision=None):
    return lax.dot_general(
        a, b, (((1,), (1,)), ((), ())), precision=precision, preferred_element_type=F32
    )


def prep_kernel(fluid, phase, cell, owner, node, proj, struct, out, pay):
    pay[...] = jnp.zeros_like(pay)
    for h in range(2):
        span = pl.ds(h * L, L)
        index = jnp.broadcast_to(cell[:, span], (8, L))
        lane, chunk = index & (L - 1), index >> 7
        for t in range(NT):
            got = lanes_of(fluid[t, :, pl.ds(0, L)], lane)
            for c in range(1, 4):
                got = jnp.where(chunk == c, lanes_of(fluid[t, :, pl.ds(c * L, L)], lane), got)
            for k in range(3):
                f = k * NT + t
                row = f // 6 * 8 + f % 6
                pay[pl.ds(row, 1), span] = jnp.sum(proj[k, :, span] * got, axis=0, keepdims=True)
    pay[pl.ds(27, 1), :] = (node[...] + 1).astype(F32)
    own = owner[...]
    hot = jnp.where(iota((64, 256), 0) == own, 1.0, 0.0)
    before = jnp.where(iota((256, 256), 0) < iota((256, 256), 1), 1.0, 0.0).astype(BF16)
    counts = jnp.dot(hot.astype(BF16), before, preferred_element_type=F32)
    rank = jnp.sum(hot * counts, axis=0, keepdims=True)
    slot = own * CAP + rank.astype(jnp.int32)
    slot_hot = jnp.where(iota((1024, 256), 0) == slot, 1.0, 0.0).astype(BF16)
    slotted = dot_nt(thirds(pay[...]), slot_hot)
    slotted = slotted[0:32] + slotted[32:64] + slotted[64:96]

    part = phase[0] * fluid[0]
    for t in range(1, NT):
        part = part + phase[t] * fluid[t]
    part = jnp.sum(part, axis=0, keepdims=True)
    part = part[:, 0:L] + part[:, L : 2 * L] + part[:, 2 * L : 3 * L] + part[:, 3 * L : 4 * L]
    part = part + pltpu.roll(part, 64, 1)
    part = part + pltpu.roll(part, 32, 1)
    is_phase = iota((8, L), 0) == 4
    place = iota((8, L), 1) >> 5
    for c in range(8):
        groups = [slotted[g * 8 : g * 8 + 8, c * L : c * L + L] for g in range(4)]
        groups[3] = jnp.where(is_phase, part, groups[3])
        turned = []
        for d in range(4):
            mixed = groups[d]
            for j in range(1, 4):
                mixed = jnp.where(place == j, groups[(j + d) % 4], mixed)
            turned.append(pltpu.roll(mixed, 32 * d, 1) if d else mixed)
        for j in range(4):
            packed = turned[(0 - j) % 4]
            for g in range(1, 4):
                packed = jnp.where(place == g, turned[(g - j) % 4], packed)
            base = (c * 4 + j) * ROWS
            for k in range(3):
                out[pl.ds(base + k * NT, NT), :] = struct[k]
            out[pl.ds(base + 21, 6), :] = packed[0:6]


def window_kernel(
    fluid, before, after, jac, nbr, freq, struct, stiff, mass, scal, flux, part, gathered
):
    omega, dfreq = scal[0], scal[1]
    for i in range(4):
        span = pl.ds(i * L, L)
        for f in range(NF):
            off = jnp.broadcast_to(nbr[pl.ds(f, 1), span], (8, L))
            place = iota((8, L), 1) + L + off
            lane = place & (L - 1)
            which = jnp.where(off == 0, 3, place >> 7)
            for t in range(NT):
                got = jnp.zeros((8, L), F32)
                for q in range(3):
                    j = i + q
                    if j == 0:
                        src = before[t]
                    elif j == 5:
                        src = after[t]
                    else:
                        src = fluid[t, :, pl.ds((j - 1) * L, L)]
                    got = jnp.where(which == q, lanes_of(src, lane), got)
                gathered[f, t] = got
        low_half = [(iota((8, L), 0) & s) == 0 for s in (4, 2, 1)]
        for t in range(NT):
            here = fluid[t, :, span]
            sums = [None] * 8
            for f in range(NF + 1):
                val = here if f == 0 else gathered[f - 1, t]
                for vv in range(4):
                    pair = jac[f, pl.ds(vv * 16, 16), span].astype(F32)
                    for u in range(2):
                        term = pair[u * 8 : u * 8 + 8] * val
                        v = vv * 2 + u
                        sums[v] = term if sums[v] is None else sums[v] + term
            level = sums
            for s, low in zip((4, 2, 1), low_half):
                half = len(level) // 2
                level = [
                    jnp.where(
                        low,
                        level[v] + pltpu.roll(level[v], 8 - s, 0),
                        level[v + half] + pltpu.roll(level[v + half], s, 0),
                    )
                    for v in range(half)
                ]
            total = level[0]
            turn = None
            for s in range(NT):
                if s != t:
                    term = float(SPECTRAL[t, s]) * fluid[s, :, span]
                    turn = term if turn is None else turn + term
            flux[t, :, span] = total + omega * turn + dfreq * freq[t, :, span]
    for k in range(3):
        acc = None
        for q in range(3):
            term = dot_nt(struct[q], stiff[k, q], lax.Precision.HIGHEST)
            acc = term if acc is None else acc + term
        for t in range(NT):
            turn = None
            for s in range(NT):
                term = float(SECOND[t, s]) * struct[k, pl.ds(s, 1), :]
                turn = term if turn is None else turn + term
            part[k, pl.ds(t, 1), :] = acc[t : t + 1] + omega * omega * mass[pl.ds(k, 1), :] * turn


def lookup_kernel(mine, other, owner, node, xyz, core, out):
    q = core[0]
    for h in range(2):
        span = pl.ds(h * L, L)
        own = jnp.broadcast_to(owner[:, span], (8, L))
        lane = jnp.broadcast_to(node[:, span], (8, L))
        chip = own >> 1
        same = (own & 1) == q
        found = [jnp.zeros((8, L), F32) for _ in range(3)]
        for table, key in (
            (mine, jnp.where(same, chip, -1)),
            (other, jnp.where(same, -1, chip)),
        ):
            for p in range(CHIPS):
                hit = key == p
                for k in range(3):
                    values = table[pl.ds(p * ROWS + k * NT, 8), :]
                    found[k] = jnp.where(hit, lanes_of(values, lane), found[k])
        last = iota((8, L), 0) == 7
        for k in range(3):
            centre = jnp.broadcast_to(xyz[pl.ds(k, 1), span], (8, L))
            out[pl.ds(k * 8, 8), span] = jnp.where(last, centre, found[k])
    sums = []
    for table in (mine, other):
        acc = table[pl.ds(25, 1), :]
        for p in range(1, CHIPS):
            acc = acc + table[pl.ds(p * ROWS + 25, 1), :]
        sums.append(acc)
    total = jnp.broadcast_to(sums[0] + sums[1], (8, L))
    out[pl.ds(24, 8), pl.ds(0, L)] = total
    out[pl.ds(24, 8), pl.ds(L, L)] = total


def loads_kernel(mine, other, part, core, out, dense):
    q = core[0]
    block = iota((8, L), 1) >> 4
    for a, table in enumerate((mine, other)):
        for c in range(4):
            shifted = []
            for i in range(8):
                values = table[pl.ds((c * 8 + i) * ROWS + 19, 8), :]
                shifted.append(jnp.where(q == 1, pltpu.roll(values, L - 16, 1), values))
            for g in range(4):
                packed = None
                for i in range(8):
                    turn = (16 * i - 32 * g) % L
                    moved = pltpu.roll(shifted[i], turn, 1) if turn else shifted[i]
                    packed = moved if packed is None else jnp.where(block == i, moved, packed)
                dense[pl.ds(g * 8, 8), pl.ds((a * 4 + c) * L, L)] = packed
    tags = dense[pl.ds(29, 1), :].astype(jnp.int32)
    node_hot = jnp.where(iota((L, 1024), 0) + 1 == tags, 1.0, 0.0).astype(BF16)
    loads = dot_nt(thirds(dense[...]), node_hot)
    loads = loads[0:32] + loads[32:64] + loads[64:96]
    for k in range(3):
        for t in range(NT):
            f = k * NT + t
            row = f // 6 * 8 + f % 6 + 2
            out[k, pl.ds(t, 1), :] = part[k, pl.ds(t, 1), :] - loads[row : row + 1]


def final_kernel(d0, d1, d2, d3, cells, sens, flux, out, phase_out):
    cols = jnp.concatenate([cells[...], jnp.zeros((5, 512), F32)], axis=0).T
    moved = None
    for ref in (d0, d1, d2, d3):
        squared = None
        for k in range(3):
            gap = cols[:, k : k + 1] - ref[pl.ds(k * 8 + 7, 1), :]
            squared = gap * gap if squared is None else squared + gap * gap
        dist = jnp.sqrt(squared)
        fall = jnp.maximum(1.0 - dist, 0.0)
        fall = fall * fall
        basis = fall * fall * (4.0 * dist + 1.0)
        high = basis.astype(BF16)
        low = (basis - high.astype(F32)).astype(BF16)
        shift = ref[pl.ds(0, 24), :]
        s_high = shift.astype(BF16)
        s_low = (shift - s_high.astype(F32)).astype(BF16)
        both = dot_nt(jnp.concatenate([s_high, s_low], axis=0), high)
        term = both[0:24] + both[24:48] + dot_nt(s_high, low)
        moved = term if moved is None else moved + term
    for t in range(NT):
        total = flux[t]
        for k in range(3):
            total = total + sens[k] * moved[k * 8 + t : k * 8 + t + 1]
        out[t] = total
    row = pl.ds(24, 1), pl.ds(0, L)
    total = (d0[row] + d2[row]) + (d1[row] + d3[row])
    total = jnp.where(iota((1, L), 1) >= 96, total, 0.0)
    phase_out[0, 0] = jnp.sum(total)


VM = pl.BlockSpec(memory_space=pltpu.VMEM)
SM = pl.BlockSpec(memory_space=pltpu.SMEM)


def kernel(body, name, ins, shapes, outs=None, scratch=(), flops=1000, size=100000):
    return pl.pallas_call(
        body,
        out_shape=[jax.ShapeDtypeStruct(s, F32) for s in shapes],
        in_specs=ins,
        out_specs=outs or [VM] * len(shapes),
        scratch_shapes=list(scratch),
        name=name,
        compiler_params=pltpu.CompilerParams(vmem_limit_bytes=32 * 1024 * 1024),
        cost_estimate=pl.CostEstimate(flops=flops, bytes_accessed=size, transcendentals=0),
    )


def on_device(
    fluid_delta,
    jacobian,
    face_nbr,
    freq_col,
    grid_sens,
    cell_xyz,
    surf_cell,
    surf_owner,
    surf_node,
    load_proj,
    surf_xyz,
    struct_delta,
    stiffness,
    mass,
    omega,
    freq_delta,
    phase_row,
):
    sections = lax.axis_size("sec")
    columns = lax.axis_size("cell")
    both = sections * columns
    struct = jnp.transpose(struct_delta, (1, 0, 2))
    stiff = jnp.transpose(stiffness, (0, 2, 1, 3))
    sens = jnp.transpose(grid_sens, (1, 0, 2))
    owner = surf_owner.reshape(1, 256)
    node = surf_node.reshape(1, 256)
    cell = surf_cell.reshape(1, 256)
    core = (lax.axis_index("sec") % 2).astype(jnp.int32).reshape(1)
    scal = jnp.concatenate([omega, freq_delta])

    (message,) = kernel(
        prep_kernel, "prep", [VM] * 7, [(CHIPS * ROWS, L)], scratch=[pltpu.VMEM((32, 256), F32)]
    )(fluid_delta, phase_row, cell, owner, node, load_proj, struct)
    groups = [[2 * i + c for i in range(sections // 2)] for c in range(2)]
    mine = lax.all_to_all(
        message.reshape(CHIPS, 1, ROWS * L), "sec", 0, 0, axis_index_groups=groups, tiled=True
    ).reshape(CHIPS * ROWS, L)
    up = [(i, i + 1) for i in range(both - 1)]
    down = [(i + 1, i) for i in range(both - 1)]
    before = lax.ppermute(fluid_delta[:, :, 3 * L :], ("sec", "cell"), up)
    after = lax.ppermute(fluid_delta[:, :, :L], ("sec", "cell"), down)
    flux, part = kernel(
        window_kernel,
        "window",
        [VM] * 9 + [SM],
        [(NT, NV, 512), (3, NT, L)],
        scratch=[pltpu.VMEM((NF, NT, 8, L), F32)],
        flops=10**9,
        size=4 * 10**6,
    )(
        fluid_delta,
        before,
        after,
        jacobian.reshape(NF + 1, 64, 512),
        face_nbr,
        freq_col,
        struct,
        stiff,
        mass,
        scal,
    )
    other = lax.ppermute(mine, "sec", [(i, i ^ 1) for i in range(sections)])
    (disp,) = kernel(lookup_kernel, "lookup", [VM] * 5 + [SM], [(32, 256)])(
        mine, other, owner, node, surf_xyz, core
    )
    d1, d3, d2 = (
        lax.ppermute(disp, "cell", [(i, (i + k) % columns) for i in range(columns)])
        for k in (1, 3, 2)
    )
    (struct_out,) = kernel(
        loads_kernel,
        "loads",
        [VM] * 3 + [SM],
        [(3, NT, L)],
        scratch=[pltpu.VMEM((32, 1024), F32)],
        size=2 * 10**6,
    )(mine, other, part, core)
    fluid_out, phase_out = kernel(
        final_kernel, "final", [VM] * 7, [(NT, NV, 512), (1, 1)], outs=[VM, SM]
    )(disp, d1, d2, d3, cell_xyz, sens, flux)
    return fluid_out, jnp.transpose(struct_out, (1, 0, 2)), phase_out.reshape(1)


def solution(mesh):
    split = ("sec", "cell")
    return jax.shard_map(
        on_device,
        mesh=mesh,
        in_specs=(
            P(None, None, split),
            P(None, None, None, split),
            P(None, split),
            P(None, None, split),
            P(None, None, split),
            P(None, split),
            P(split),
            P(split, None),
            P(split),
            P(None, None, split),
            P(None, split),
            P(None, None, split),
            P(None, None, None, split),
            P(None, split),
            P(),
            P(),
            P(None, None, split),
        ),
        out_specs=(P(None, None, split), P(None, None, split), P()),
        check_vma=False,
    )
```

profile of v0, /device:TPU:1, one launch (start us, length us, event | category | flops | bytes accessed | tf_op | source)
XLA Modules:
  0.0 55.2 jit_solution(14325169701214657555)
XLA Ops:
  0.7 0.7 %copy-done.10 = s32[256]{0:T(256)S(1)} copy-done((s32[256]{0:T(256)S(1)}, s32[256]{0:T(256)}, u32[]{:S(2)}) %copy-start.10) | copy-done | bytes 1048
  1.3 0.0 copy-done.11
  1.3 0.0 copy-done.9
  1.3 0.9 %copy-done = f32[7,8,512]{2,1,0:T(8,128)S(1)} copy-done((f32[7,8,512]{2,1,0:T(8,128)S(1)}, f32[7,8,512]{2,1,0:T(8,128)}, u32[]{:S(2)}) %copy-start) | copy-done | bytes 114712
  2.2 0.9 %copy-done.2 = f32[7,8,512]{2,1,0:T(8,128)S(1)} copy-done((f32[7,8,512]{2,1,0:T(8,128)S(1)}, f32[7,8,512]{2,1,0:T(8,128)}, u32[]{:S(2)}) %copy-start.2) | copy-done | bytes 114712
  3.1 0.7 %copy-done.4 = f32[3,8,256]{2,1,0:T(8,128)S(1)} copy-done((f32[3,8,256]{2,1,0:T(8,128)S(1)}, f32[3,8,256]{2,1,0:T(8,128)}, u32[]{:S(2)}) %copy-start.4) | copy-done | bytes 24600
  3.9 0.7 %copy-done.5 = f32[7,3,128]{2,0,1:T(8,128)S(1)} copy-done((f32[7,3,128]{2,0,1:T(8,128)S(1)}, f32[7,3,128]{2,0,1:T(8,128)}, u32[]{:S(2)}) %copy-start.5) | copy-done | bytes 10776
  4.6 0.6 %prep.1 = f32[864,128]{1,0:T(8,128)S(1)} custom-call(f32[7,8,512]{2,1,0:T(8,128)S(1)} %copy-done, f32[7,8,512]{2,1,0:T(8,128)S(1)} %copy-done.2, s32[1,256]{1,0:T(1,128)S(1)} %bitcast.23, s32[1,256]{1,0:T(1,128)S(1)} %bitcast.19, s32[1,256]{1,0:T(1,128)S(1)} %bitcast.21, f32[3,8,256]{2,1,0:T(8,128)S(1)} %copy-done.4, f32[3,7,128]{2,1,0:T(8,128)S(1)} %bitcast.17), custom_call_target="tpu_custom_call" | custom-call | flops 1000 | bytes 100000 | tf_op jit(solution)/shard_map/prep/pallas_call | solution.py:315
  5.2 0.0 copy-start.12
  5.2 26.0 %all_to_all.5 = f32[32,1,3456]{2,1,0:T(1,128)S(1)} all-to-all(f32[32,1,3456]{2,1,0:T(1,128)S(1)} %bitcast.15), channel_id=1, replica_groups={{0,8,16,24,32,40,48,56,64,72,80,88,96,104,112,120,128,136,144,152,160,1..., dimensions={0} | all-to-all | bytes 884736 | tf_op jit(solution)/shard_map/all_to_all | solution.py:319
  31.1 3.1 %collective-permute-start = (f32[864,128]{1,0:T(8,128)S(1)}, f32[864,128]{1,0:T(8,128)S(1)}, u32[]{:S(2)}, u32[]{:S(2)}) collective-permute-start(f32[864,128]{1,0:T(8,128)S(1)} %bitcast.12), channel_id=1, source_target_pairs={{0,4},{4,0},{8,12},{12,8},{16,20},{20,16},{24,28},{28,24},{32,36},... | collective-permute-start | bytes 1327112 | tf_op jit(solution)/shard_map/ppermute | solution.py:346
  34.2 4.5 %collective-permute-start.5 = (f32[7,8,128]{2,1,0:T(8,128)S(1)}, f32[7,8,128]{2,1,0:T(8,128)S(1)}, u32[]{:S(2)}, u32[]{:S(2)}) collective-permute-start(f32[7,8,128]{2,1,0:T(8,128)S(1)} %get-tuple-element.11), channel_id=1, source_target_pairs={{1,0},{2,1},{3,2},{4,3},{5,4},{6,5},{7,6},{8,7},{9,8},{10,9},{11,1... | collective-permute-start | bytes 86024 | tf_op jit(solution)/shard_map/ppermute | solution.py:325
  38.7 1.9 %collective-permute-start.4 = (f32[7,8,128]{2,1,0:T(8,128)S(1)}, f32[7,8,128]{2,1,0:T(8,128)S(1)}, u32[]{:S(2)}, u32[]{:S(2)}) collective-permute-start(f32[7,8,128]{2,1,0:T(8,128)S(1)} %get-tuple-element.12), channel_id=1, source_target_pairs={{0,1},{1,2},{2,3},{3,4},{4,5},{5,6},{6,7},{7,8},{8,9},{9,10},{10,1... | collective-permute-start | bytes 86024 | tf_op jit(solution)/shard_map/ppermute | solution.py:324
  42.0 0.1 pad_maximum_fusion.scal
  42.0 0.0 collective-permute-done.other
  42.0 0.7 %copy-done.8 = f32[3,256]{1,0:T(4,128)S(1)} copy-done((f32[3,256]{1,0:T(4,128)S(1)}, f32[3,256]{1,0:T(4,128)}, u32[]{:S(2)}) %copy-start.8) | copy-done | bytes 3096
  42.7 0.0 copy-start.15
  42.7 0.5 lookup.1.d0
  43.2 0.0 copy-start.16
  43.2 4.0 %collective-permute-start.3 = (f32[32,256]{1,0:T(8,128)S(1)}, f32[32,256]{1,0:T(8,128)S(1)}, u32[]{:S(2)}, u32[]{:S(2)}) collective-permute-start(f32[32,256]{1,0:T(8,128)S(1)} %lookup.1.d0), channel_id=1, source_target_pairs={{0,3},{1,0},{2,1},{3,2},{4,7},{5,4},{6,5},{7,6},{8,11},{9,8},{10,9... | collective-permute-start | bytes 98312 | tf_op jit(solution)/shard_map/ppermute | solution.py:351
  47.3 0.0 collective-permute-start.2
  47.3 0.7 %collective-permute-start.1 = (f32[32,256]{1,0:T(8,128)S(1)}, f32[32,256]{1,0:T(8,128)S(1)}, u32[]{:S(2)}, u32[]{:S(2)}) collective-permute-start(f32[32,256]{1,0:T(8,128)S(1)} %lookup.1.d0), channel_id=1, source_target_pairs={{0,1},{1,2},{2,3},{3,0},{4,5},{5,6},{6,7},{7,4},{8,9},{9,10},{10,1... | collective-permute-start | bytes 98312 | tf_op jit(solution)/shard_map/ppermute | solution.py:351
  47.9 0.0 collective-permute-done.5.after
  47.9 0.0 collective-permute-done.4.before
  47.9 0.0 copy-done.1
  48.0 0.0 copy-done.6
  48.0 1.9 %window.1 = (f32[7,8,512]{2,1,0:T(8,128)S(1)}, f32[3,7,128]{2,1,0:T(8,128)S(1)}) custom-call(f32[7,8,512]{2,1,0:T(8,128)S(1)} %copy-done.1, f32[7,8,128]{2,1,0:T(8,128)S(1)} %collective-permute-done.4.before, f32[7,8,128]{2,1,0:T(8,128)S(1)} %collective-permute-done.5.after, bf16[7,64,512]{2,1,0:T(8,128)(2,1)S(1)} %bitcast.25, s32[6,512]{1,0:T(8,128)S(1)} %copy-done.15, ...), custom_call_target="tpu_custom_call" | custom-call | flops 1000000000 | bytes 4000000 | tf_op jit(solution)/shard_map/window/pallas_call | solution.py:326
  49.9 1.2 %loads.1 = f32[3,7,128]{2,1,0:T(8,128)} custom-call(f32[864,128]{1,0:T(8,128)S(1)} %bitcast.14, f32[864,128]{1,0:T(8,128)S(1)} %collective-permute-done.other, f32[3,7,128]{2,1,0:T(8,128)S(1)} %get-tuple-element.9.part, s32[1]{0:T(128)} %bitcast.6.core), custom_call_target="tpu_custom_call" | custom-call | flops 1000 | bytes 2000000 | tf_op jit(solution)/shard_map/loads/pallas_call | solution.py:354
  51.0 0.0 collective-permute-done.3.d3
  51.0 0.8 %collective-permute-done.2.d2 = f32[32,256]{1,0:T(8,128)S(1)} collective-permute-done((f32[32,256]{1,0:T(8,128)S(1)}, f32[32,256]{1,0:T(8,128)S(1)}, u32[]{:S(2)}, u32[]{:S(2)}) %collective-permute-start.2) | collective-permute-done | bytes 32800 | tf_op jit(solution)/shard_map/ppermute | solution.py:351
  51.9 0.4 collective-permute-done.1.d1
  52.3 2.9 %final.1 = (f32[7,8,512]{2,1,0:T(8,128)}, f32[1,1]{1,0:T(1,128)}) custom-call(f32[32,256]{1,0:T(8,128)S(1)} %lookup.1.d0, f32[32,256]{1,0:T(8,128)S(1)} %collective-permute-done.1.d1, f32[32,256]{1,0:T(8,128)S(1)} %collective-permute-done.2.d2, f32[32,256]{1,0:T(8,128)S(1)} %collective-permute-done.3.d3, f32[3,512]{1,0:T(4,128)S(1)} %copy-done.7, ...), custom_call_target="tpu_custom_call" | custom-call | flops 1000 | bytes 100000 | tf_op jit(solution)/shard_map/final/pallas_call | solution.py:362
  (22 shorter events, 0.0 us)
Async XLA Ops:
  0.6 0.7 %copy-start.10 = (s32[256]{0:T(256)S(1)}, s32[256]{0:T(256)}, u32[]{:S(2)}) copy-start(s32[256]{0:T(256)} %param.25) | copy-start | bytes 3076
  0.6 0.7 %copy-start.11 = (s32[256]{0:T(256)S(1)}, s32[256]{0:T(256)}, u32[]{:S(2)}) copy-start(s32[256]{0:T(256)} %param.23) | copy-start | bytes 3076
  0.7 0.7 %copy-start.9 = (s32[256,1]{0,1:T(1,128)S(1)}, s32[256,1]{0,1:T(1,128)}, u32[]{:S(2)}) copy-start(s32[256,1]{0,1:T(1,128)} %param.24) | copy-start | bytes 3076
  1.3 0.9 %copy-start = (f32[7,8,512]{2,1,0:T(8,128)S(1)}, f32[7,8,512]{2,1,0:T(8,128)}, u32[]{:S(2)}) copy-start(f32[7,8,512]{2,1,0:T(8,128)} %fluid.3) | copy-start | bytes 344068
  2.2 0.9 %copy-start.2 = (f32[7,8,512]{2,1,0:T(8,128)S(1)}, f32[7,8,512]{2,1,0:T(8,128)}, u32[]{:S(2)}) copy-start(f32[7,8,512]{2,1,0:T(8,128)} %phase.1) | copy-start | bytes 344068
  3.1 0.7 %copy-start.4 = (f32[3,8,256]{2,1,0:T(8,128)S(1)}, f32[3,8,256]{2,1,0:T(8,128)}, u32[]{:S(2)}) copy-start(f32[3,8,256]{2,1,0:T(8,128)} %proj.1) | copy-start | bytes 73732
  3.9 0.7 %copy-start.5 = (f32[7,3,128]{2,0,1:T(8,128)S(1)}, f32[7,3,128]{2,0,1:T(8,128)}, u32[]{:S(2)}) copy-start(f32[7,3,128]{2,0,1:T(8,128)} %param.28) | copy-start | bytes 32260
  5.2 42.8 %copy-start.12 = (f32[3,128,3,128]{3,1,2,0:T(8,128)S(1)}, f32[3,128,3,128]{3,1,2,0:T(8,128)}, u32[]{:S(2)}) copy-start(f32[3,128,3,128]{3,1,2,0:T(8,128)} %param.29) | copy-start | bytes 1769476
  31.1 10.9 %collective-permute-start = (f32[864,128]{1,0:T(8,128)S(1)}, f32[864,128]{1,0:T(8,128)S(1)}, u32[]{:S(2)}, u32[]{:S(2)}) collective-permute-start(f32[864,128]{1,0:T(8,128)S(1)} %bitcast.12), channel_id=1, source_target_pairs={{0,4},{4,0},{8,12},{12,8},{16,20},{20,16},{24,28},{28,24},{32,36},... | collective-permute-start | bytes 1327112 | tf_op jit(solution)/shard_map/ppermute | solution.py:346
  34.2 13.7 %collective-permute-start.5 = (f32[7,8,128]{2,1,0:T(8,128)S(1)}, f32[7,8,128]{2,1,0:T(8,128)S(1)}, u32[]{:S(2)}, u32[]{:S(2)}) collective-permute-start(f32[7,8,128]{2,1,0:T(8,128)S(1)} %get-tuple-element.11), channel_id=1, source_target_pairs={{1,0},{2,1},{3,2},{4,3},{5,4},{6,5},{7,6},{8,7},{9,8},{10,9},{11,1... | collective-permute-start | bytes 86024 | tf_op jit(solution)/shard_map/ppermute | solution.py:325
  38.7 9.2 %collective-permute-start.4 = (f32[7,8,128]{2,1,0:T(8,128)S(1)}, f32[7,8,128]{2,1,0:T(8,128)S(1)}, u32[]{:S(2)}, u32[]{:S(2)}) collective-permute-start(f32[7,8,128]{2,1,0:T(8,128)S(1)} %get-tuple-element.12), channel_id=1, source_target_pairs={{0,1},{1,2},{2,3},{3,4},{4,5},{5,6},{6,7},{7,8},{8,9},{9,10},{10,1... | collective-permute-start | bytes 86024 | tf_op jit(solution)/shard_map/ppermute | solution.py:324
  42.0 0.7 %copy-start.8 = (f32[3,256]{1,0:T(4,128)S(1)}, f32[3,256]{1,0:T(4,128)}, u32[]{:S(2)}) copy-start(f32[3,256]{1,0:T(4,128)} %xyz.1) | copy-start | bytes 9220
  42.7 5.2 %copy-start.1 = (f32[7,8,512]{2,1,0:T(8,128)S(1)}, f32[7,8,512]{2,1,0:T(8,128)}, u32[]{:S(2)}) copy-start(f32[7,8,512]{2,1,0:T(8,128)} %fluid.3) | copy-start | bytes 344068
  42.7 5.2 %copy-start.6 = (f32[7,3,128]{2,0,1:T(8,128)S(1)}, f32[7,3,128]{2,0,1:T(8,128)}, u32[]{:S(2)}) copy-start(f32[7,3,128]{2,0,1:T(8,128)} %param.28) | copy-start | bytes 32260
  42.7 5.2 %copy-start.13 = (bf16[7,8,8,512]{3,2,1,0:T(8,128)(2,1)S(1)}, bf16[7,8,8,512]{3,2,1,0:T(8,128)(2,1)}, u32[]{:S(2)}) copy-start(bf16[7,8,8,512]{3,2,1,0:T(8,128)(2,1)} %param.18) | copy-start | bytes 1376260
  42.7 5.2 %copy-start.14 = (f32[7,8,512]{2,1,0:T(8,128)S(1)}, f32[7,8,512]{2,1,0:T(8,128)}, u32[]{:S(2)}) copy-start(f32[7,8,512]{2,1,0:T(8,128)} %freq.1) | copy-start | bytes 344068
  42.7 5.3 %copy-start.15 = (s32[6,512]{1,0:T(8,128)S(1)}, s32[6,512]{1,0:T(8,128)}, u32[]{:S(2)}) copy-start(s32[6,512]{1,0:T(8,128)} %nbr.1) | copy-start | bytes 36868
  43.2 4.8 %copy-start.16 = (f32[3,128]{1,0:T(4,128)S(1)}, f32[3,128]{1,0:T(4,128)}, u32[]{:S(2)}) copy-start(f32[3,128]{1,0:T(4,128)} %mass.1) | copy-start | bytes 4612
  43.2 7.8 %collective-permute-start.3 = (f32[32,256]{1,0:T(8,128)S(1)}, f32[32,256]{1,0:T(8,128)S(1)}, u32[]{:S(2)}, u32[]{:S(2)}) collective-permute-start(f32[32,256]{1,0:T(8,128)S(1)} %lookup.1.d0), channel_id=1, source_target_pairs={{0,3},{1,0},{2,1},{3,2},{4,7},{5,4},{6,5},{7,6},{8,11},{9,8},{10,9... | collective-permute-start | bytes 98312 | tf_op jit(solution)/shard_map/ppermute | solution.py:351
  47.3 4.6 %collective-permute-start.2 = (f32[32,256]{1,0:T(8,128)S(1)}, f32[32,256]{1,0:T(8,128)S(1)}, u32[]{:S(2)}, u32[]{:S(2)}) collective-permute-start(f32[32,256]{1,0:T(8,128)S(1)} %lookup.1.d0), channel_id=1, source_target_pairs={{0,2},{1,3},{2,0},{3,1},{4,6},{5,7},{6,4},{7,5},{8,10},{9,11},{10,... | collective-permute-start | bytes 98312 | tf_op jit(solution)/shard_map/ppermute | solution.py:351
  47.3 5.0 %collective-permute-start.1 = (f32[32,256]{1,0:T(8,128)S(1)}, f32[32,256]{1,0:T(8,128)S(1)}, u32[]{:S(2)}, u32[]{:S(2)}) collective-permute-start(f32[32,256]{1,0:T(8,128)S(1)} %lookup.1.d0), channel_id=1, source_target_pairs={{0,1},{1,2},{2,3},{3,0},{4,5},{5,6},{6,7},{7,4},{8,9},{9,10},{10,1... | collective-permute-start | bytes 98312 | tf_op jit(solution)/shard_map/ppermute | solution.py:351
  49.9 2.4 %copy-start.3 = (f32[8,3,512]{2,0,1:T(8,128)S(1)}, f32[8,3,512]{2,0,1:T(8,128)}, u32[]{:S(2)}) copy-start(f32[8,3,512]{2,0,1:T(8,128)} %param.21) | copy-start | bytes 147460
  49.9 2.4 %copy-start.7 = (f32[3,512]{1,0:T(4,128)S(1)}, f32[3,512]{1,0:T(4,128)}, u32[]{:S(2)}) copy-start(f32[3,512]{1,0:T(4,128)} %cells.1) | copy-start | bytes 18436
where the time goes:
time: 55.6 us; the launch traced here: 55.2 us
  blocking collectives  26 us (47%)
  starting transfers between devices  14.2 us (26%)
  Pallas kernels  6.99 us (13%)
  local copies, waits for them, and re-layouts  4.66 us (8%)
  between operations  2.08 us (4%)
  waiting for transfers between devices  1.26 us (2%)
    all_to_all x1, blocking collectives, on_device(): lax.all_to_all(message.reshape(CHIPS, 1, ROWS * L), 'sec', 0, 0, axis_ind...  26 us
    ppermute x3, starting transfers between devices, on_device(): lax.ppermute(disp, 'cell', [(i, (i + k) % columns) for i in range(columns)])  4.7 us
    unnamed x34, local copies, waits for them, and re-layouts  4.65 us
    ppermute x1, starting transfers between devices, on_device(): after = lax.ppermute(fluid_delta[:, :, :L], ('sec', 'cell'), down)  4.54 us
    ppermute x1, starting transfers between devices, on_device(): other = lax.ppermute(mine, 'sec', [(i, i ^ 1) for i in range(sections)])  3.05 us
    pallas_call x1, Pallas kernels, on_device(): kernel(final_kernel, 'final', [VM] * 7, [(NT, NV, 512), (1, 1)], outs=[VM...  2.93 us
    ppermute x1, starting transfers between devices, on_device(): before = lax.ppermute(fluid_delta[:, :, 3 * L:], ('sec', 'cell'), up)  1.92 us
    pallas_call x1, Pallas kernels, on_device(): kernel(window_kernel, 'window', [VM] * 9 + [SM], [(NT, NV, 512), (3, NT,...  1.86 us
  transfers between devices with their start and end apart: 6, of which 2 were waited for; matrix products, arithmetic and copies ran while one was open for 0% of the time, Pallas kernels for 6%

commit v1 on v0

--- a/solution.py
+++ b/solution.py
@@ -54,8 +54,15 @@
     )
 
 
-def prep_kernel(fluid, phase, cell, owner, node, proj, struct, out, pay):
+def prep_kernel(*refs):
+    far, out, pay, near, sems = refs[:7], refs[7], refs[8], refs[9:16], refs[16]
+    fluid, phase, cell, owner, node, proj, struct = near
+    copies = [pltpu.make_async_copy(a, b, sems.at[i]) for i, (a, b) in enumerate(zip(far, near))]
+    for i in (2, 3, 4, 0, 5, 1, 6):
+        copies[i].start()
     pay[...] = jnp.zeros_like(pay)
+    for i in (2, 3, 4, 0, 5, 1, 6):
+        copies[i].wait()
     for h in range(2):
         span = pl.ds(h * L, L)
         index = jnp.broadcast_to(cell[:, span], (8, L))
@@ -233,30 +240,69 @@
             out[k, pl.ds(t, 1), :] = part[k, pl.ds(t, 1), :] - loads[row : row + 1]
 
 
-def final_kernel(d0, d1, d2, d3, cells, sens, flux, out, phase_out):
-    cols = jnp.concatenate([cells[...], jnp.zeros((5, 512), F32)], axis=0).T
-    moved = None
-    for ref in (d0, d1, d2, d3):
-        squared = None
-        for k in range(3):
-            gap = cols[:, k : k + 1] - ref[pl.ds(k * 8 + 7, 1), :]
-            squared = gap * gap if squared is None else squared + gap * gap
-        dist = jnp.sqrt(squared)
+def parts_of(values):
+    high = values.astype(BF16).astype(F32)
+    rest = values - high
+    middle = rest.astype(BF16).astype(F32)
+    return high, middle, rest - middle
+
+
+def features(xyz, scale, ones_first, out):
+    at = 0
+    square = None
+    for point in xyz:
+        square = point * point if square is None else square + point * point
+        p = [scale * part for part in parts_of(point)]
+        order = (0, 0, 1, 1, 0, 2) if ones_first else (0, 1, 0, 1, 2, 0)
+        for i in order:
+            out[pl.ds(at, 1), :] = p[i]
+            at += 1
+    one = jnp.ones_like(square)
+    squares = list(parts_of(square))
+    for row in [one] * 3 + squares if ones_first else squares + [one] * 3:
+        out[pl.ds(at, 1), :] = row
+        at += 1
+    out[pl.ds(24, 8), :] = jnp.zeros((8, square.shape[1]), F32)
+
+
+def move_by(ref, cols, rows, squared, basis):
+    features([ref[pl.ds(k * 8 + 7, 1), :] for k in range(3)], -2.0, True, rows)
+    squared[...] = jnp.dot(cols, rows[...].astype(BF16), preferred_element_type=F32)
+    for c in range(8):
+        span = pl.ds(c * 64, 64)
+        gap = jnp.maximum(squared[span, :], 1e-30)
+        dist = gap * lax.rsqrt(gap)
         fall = jnp.maximum(1.0 - dist, 0.0)
         fall = fall * fall
-        basis = fall * fall * (4.0 * dist + 1.0)
-        high = basis.astype(BF16)
-        low = (basis - high.astype(F32)).astype(BF16)
-        shift = ref[pl.ds(0, 24), :]
-        s_high = shift.astype(BF16)
-        s_low = (shift - s_high.astype(F32)).astype(BF16)
-        both = dot_nt(jnp.concatenate([s_high, s_low], axis=0), high)
-        term = both[0:24] + both[24:48] + dot_nt(s_high, low)
-        moved = term if moved is None else moved + term
+        value = fall * fall * (4.0 * dist + 1.0)
+        high = value.astype(BF16)
+        basis[span, pl.ds(0, 256)] = high
+        basis[span, pl.ds(256, 256)] = (value - high.astype(F32)).astype(BF16)
+    shift = ref[pl.ds(0, 24), :]
+    high = shift.astype(BF16).astype(F32)
+    both = jnp.concatenate([high, shift - high], axis=0).astype(BF16)
+    low = jnp.concatenate([high, jnp.zeros_like(high)], axis=0).astype(BF16)
+    return dot_nt(basis[...], jnp.concatenate([both, low], axis=1))
+
+
+def own_kernel(d0, cells, cols, moved, feats, rows, squared, basis):
+    features([cells[pl.ds(k, 1), :] for k in range(3)], 1.0, False, feats)
+    turned = feats[...].T
+    cols[...] = turned
+    moved[...] = move_by(d0, turned.astype(BF16), rows, squared, basis)
+
+
+def final_kernel(d0, d1, d2, d3, cols, moved, sens, flux, out, phase_out, *scratch):
+    near = cols[...].astype(BF16)
+    total = moved[...]
+    for i, ref in enumerate((d1, d3, d2)):
+        total = total + move_by(ref, near, *scratch[3 * i : 3 * i + 3])
+    turned = total.T
+    motion = turned[0:24] + turned[24:48]
     for t in range(NT):
         total = flux[t]
         for k in range(3):
-            total = total + sens[k] * moved[k * 8 + t : k * 8 + t + 1]
+            total = total + sens[k] * motion[k * 8 + t : k * 8 + t + 1]
         out[t] = total
     row = pl.ds(24, 1), pl.ds(0, L)
     total = (d0[row] + d2[row]) + (d1[row] + d3[row])
@@ -265,10 +311,11 @@
 
 
 VM = pl.BlockSpec(memory_space=pltpu.VMEM)
+HBM = pl.BlockSpec(memory_space=pltpu.HBM)
 SM = pl.BlockSpec(memory_space=pltpu.SMEM)
 
 
-def kernel(body, name, ins, shapes, outs=None, scratch=(), flops=1000, size=100000):
+def kernel(body, name, ins, shapes, outs=None, scratch=(), size=100000, vmem=32):
     return pl.pallas_call(
         body,
         out_shape=[jax.ShapeDtypeStruct(s, F32) for s in shapes],
@@ -276,8 +323,8 @@
         out_specs=outs or [VM] * len(shapes),
         scratch_shapes=list(scratch),
         name=name,
-        compiler_params=pltpu.CompilerParams(vmem_limit_bytes=32 * 1024 * 1024),
-        cost_estimate=pl.CostEstimate(flops=flops, bytes_accessed=size, transcendentals=0),
+        compiler_params=pltpu.CompilerParams(vmem_limit_bytes=vmem * 1024 * 1024),
+        cost_estimate=pl.CostEstimate(flops=1000, bytes_accessed=size, transcendentals=0),
     )
 
 
@@ -313,7 +360,22 @@
     scal = jnp.concatenate([omega, freq_delta])
 
     (message,) = kernel(
-        prep_kernel, "prep", [VM] * 7, [(CHIPS * ROWS, L)], scratch=[pltpu.VMEM((32, 256), F32)]
+        prep_kernel,
+        "prep",
+        [HBM] * 7,
+        [(CHIPS * ROWS, L)],
+        scratch=[
+            pltpu.VMEM((32, 256), F32),
+            pltpu.VMEM((NT, NV, 512), F32),
+            pltpu.VMEM((NT, NV, 512), F32),
+            pltpu.VMEM((1, 256), jnp.int32),
+            pltpu.VMEM((1, 256), jnp.int32),
+            pltpu.VMEM((1, 256), jnp.int32),
+            pltpu.VMEM((3, NV, 256), F32),
+            pltpu.VMEM((3, NT, L), F32),
+            pltpu.SemaphoreType.DMA((7,)),
+        ],
+        vmem=60,
     )(fluid_delta, phase_row, cell, owner, node, load_proj, struct)
     groups = [[2 * i + c for i in range(sections // 2)] for c in range(2)]
     mine = lax.all_to_all(
@@ -329,7 +391,6 @@
         [VM] * 9 + [SM],
         [(NT, NV, 512), (3, NT, L)],
         scratch=[pltpu.VMEM((NF, NT, 8, L), F32)],
-        flops=10**9,
         size=4 * 10**6,
     )(
         fluid_delta,
@@ -343,6 +404,7 @@
         mass,
         scal,
     )
+    mine, flux, part = lax.optimization_barrier((mine, flux, part))
     other = lax.ppermute(mine, "sec", [(i, i ^ 1) for i in range(sections)])
     (disp,) = kernel(lookup_kernel, "lookup", [VM] * 5 + [SM], [(32, 256)])(
         mine, other, owner, node, surf_xyz, core
@@ -359,9 +421,27 @@
         scratch=[pltpu.VMEM((32, 1024), F32)],
         size=2 * 10**6,
     )(mine, other, part, core)
+    move = [
+        pltpu.VMEM((32, 256), F32),
+        pltpu.VMEM((512, 256), F32),
+        pltpu.VMEM((512, 512), BF16),
+    ]
+    cols, moved = kernel(
+        own_kernel,
+        "own",
+        [VM] * 2,
+        [(512, 32), (512, 48)],
+        scratch=[pltpu.VMEM((32, 512), F32)] + move,
+        size=2 * 10**6,
+    )(disp, cell_xyz)
     fluid_out, phase_out = kernel(
-        final_kernel, "final", [VM] * 7, [(NT, NV, 512), (1, 1)], outs=[VM, SM]
-    )(disp, d1, d2, d3, cell_xyz, sens, flux)
+        final_kernel,
+        "final",
+        [VM] * 8,
+        [(NT, NV, 512), (1, 1)],
+        outs=[VM, SM],
+        scratch=move * 3,
+    )(disp, d1, d2, d3, cols, moved, sens, flux)
     return fluid_out, jnp.transpose(struct_out, (1, 0, 2)), phase_out.reshape(1)
 
 

time: 55.6 us -> 44.1 us (0.79)
  blocking collectives: 26 us -> 0 us
  starting transfers between devices: 14.2 us -> 26.4 us
  waiting for transfers between devices: 1.26 us -> 6.54 us
  local copies, waits for them, and re-layouts: 4.66 us -> 0.07 us
  Pallas kernels: 6.99 us -> 8.67 us
    all_to_all x1 -> x0, blocking collectives: 26 us -> none  [on_device(): lax.all_to_all(message.reshape(CHIPS, 1, ROWS * L), 'sec', 0, 0, axis_ind...]
    all_to_all x0 -> x1, starting transfers between devices: none -> 12 us  [on_device(): lax.all_to_all(message.reshape(CHIPS, 1, ROWS * L), 'sec', 0, 0, axis_ind...]
    unnamed x34 -> x24, local copies, waits for them, and re-layouts: 4.65 us -> 0.06 us
    ppermute x1, waiting for transfers between devices: 0.01 us -> 3.39 us  [on_device(): before = lax.ppermute(fluid_delta[:, :, 3 * L:], ('sec', 'cell'), up)]
    pallas_call x2 -> x3, Pallas kernels: 3.48 us -> 5.17 us  [the longest x1 2.46 us: on_device(): kernel(prep_kernel, 'prep', [HBM] * 7, [(CHIPS * ROWS, L)], scratch=[pltp...]
    ppermute x1, waiting for transfers between devices: 0.01 us -> 1.41 us  [on_device(): other = lax.ppermute(mine, 'sec', [(i, i ^ 1) for i in range(sections)])]
    ppermute x1, starting transfers between devices: 4.54 us -> 5.62 us  [on_device(): after = lax.ppermute(fluid_delta[:, :, :L], ('sec', 'cell'), down)]
    ppermute x3, starting transfers between devices: 4.7 us -> 3.85 us  [on_device(): lax.ppermute(disp, 'cell', [(i, (i + k) % columns) for i in range(columns)])]
  transfers between devices with their start and end apart: 6 -> 7, of which waited for: 2 -> 4; matrix products, arithmetic and copies ran while one was open for 0% -> 0% of each run, Pallas kernels for 6% -> 8%
where the time goes in v1:
time: 44.1 us; the launch traced here: 43.8 us
  starting transfers between devices  26.4 us (60%)
  Pallas kernels  8.67 us (20%)
  waiting for transfers between devices  6.54 us (15%)
  between operations  2.09 us (5%)
    all_to_all x1, starting transfers between devices, on_device(): lax.all_to_all(message.reshape(CHIPS, 1, ROWS * L), 'sec', 0, 0, axis_ind...  12 us
    ppermute x1, starting transfers between devices, on_device(): after = lax.ppermute(fluid_delta[:, :, :L], ('sec', 'cell'), down)  5.62 us
    ppermute x3, starting transfers between devices, on_device(): lax.ppermute(disp, 'cell', [(i, (i + k) % columns) for i in range(columns)])  3.85 us
    ppermute x1, waiting for transfers between devices, on_device(): before = lax.ppermute(fluid_delta[:, :, 3 * L:], ('sec', 'cell'), up)  3.39 us
    ppermute x1, starting transfers between devices, on_device(): other = lax.ppermute(mine, 'sec', [(i, i ^ 1) for i in range(sections)])  2.96 us
    pallas_call x1, Pallas kernels, on_device(): kernel(prep_kernel, 'prep', [HBM] * 7, [(CHIPS * ROWS, L)], scratch=[pltp...  2.46 us
    pallas_call x1, Pallas kernels, on_device(): kernel(final_kernel, 'final', [VM] * 8, [(NT, NV, 512), (1, 1)], outs=[VM...  2.04 us
    ppermute x1, starting transfers between devices, on_device(): before = lax.ppermute(fluid_delta[:, :, 3 * L:], ('sec', 'cell'), up)  1.92 us
  transfers between devices with their start and end apart: 7, of which 4 were waited for; matrix products, arithmetic and copies ran while one was open for 0% of the time, Pallas kernels for 8%

profile of v1, /device:TPU:1, one launch (start us, length us, event | category | flops | bytes accessed | tf_op | source)
XLA Modules:
  0.0 43.8 jit_solution(732740491718501618)
XLA Ops:
  0.6 0.0 copy-start.2
  0.6 2.5 %prep.1 = f32[864,128]{1,0:T(8,128)} custom-call(f32[7,8,512]{2,1,0:T(8,128)} %fluid.1, f32[7,8,512]{2,1,0:T(8,128)} %refs_1_.1, s32[1,256]{1,0:T(1,128)} %bitcast.26, s32[1,256]{1,0:T(1,128)} %bitcast.20, s32[1,256]{1,0:T(1,128)} %bitcast.22, f32[3,8,256]{2,1,0:T(8,128)} %refs_5_.1, f32[3,7,128]{2,1,0:T(8,128)} %bitcast.17), custom_call_target="tpu_custom_call" | custom-call | flops 1000 | bytes 100000 | tf_op jit(solution)/shard_map/prep/pallas_call | solution.py:362
  3.1 0.0 copy-start.1
  3.1 0.0 copy-start
  3.1 0.0 copy-start.6
  3.1 0.0 copy-start.11
  3.2 12.0 %all-to-all-start = ((f32[32,1,3456]{2,1,0:T(1,128)}), f32[32,1,3456]{2,1,0:T(1,128)S(1)}, u32[]{:S(2)}, u32[]{:S(2)}) async-start(f32[32,1,3456]{2,1,0:T(1,128)} %bitcast.24), calls=%async_computation | async-start | bytes 884736 | tf_op jit(solution)/shard_map/all_to_all | solution.py:381
  15.2 0.0 copy-done
  15.2 0.0 copy-start.3
  15.2 0.0 copy-start.4
  15.2 5.6 %collective-permute-start.1 = (f32[7,8,128]{2,1,0:T(8,128)S(1)}, f32[7,8,128]{2,1,0:T(8,128)S(1)}, u32[]{:S(2)}, u32[]{:S(2)}) collective-permute-start(f32[7,8,128]{2,1,0:T(8,128)S(1)} %get-tuple-element.21), channel_id=1, source_target_pairs={{1,0},{2,1},{3,2},{4,3},{5,4},{6,5},{7,6},{8,7},{9,8},{10,9},{11,1... | collective-permute-start | bytes 86024 | tf_op jit(solution)/shard_map/ppermute | solution.py:387
  20.8 1.9 %collective-permute-start = (f32[7,8,128]{2,1,0:T(8,128)S(1)}, f32[7,8,128]{2,1,0:T(8,128)S(1)}, u32[]{:S(2)}, u32[]{:S(2)}) collective-permute-start(f32[7,8,128]{2,1,0:T(8,128)S(1)} %get-tuple-element.22), channel_id=1, source_target_pairs={{0,1},{1,2},{2,3},{3,4},{4,5},{5,6},{6,7},{7,8},{8,9},{9,10},{10,1... | collective-permute-start | bytes 86024 | tf_op jit(solution)/shard_map/ppermute | solution.py:386
  24.1 0.1 pad_maximum_fusion.scal
  24.1 0.0 collective-permute-done.1.after
  24.1 3.4 %collective-permute-done.before = f32[7,8,128]{2,1,0:T(8,128)S(1)} collective-permute-done((f32[7,8,128]{2,1,0:T(8,128)S(1)}, f32[7,8,128]{2,1,0:T(8,128)S(1)}, u32[]{:S(2)}, u32[]{:S(2)}) %collective-permute-start) | collective-permute-done | bytes 28704 | tf_op jit(solution)/shard_map/ppermute | solution.py:386
  27.5 0.0 copy-done.1
  27.6 1.9 %window.1 = (f32[7,8,512]{2,1,0:T(8,128)S(1)}, f32[3,7,128]{2,1,0:T(8,128)S(1)}) custom-call(f32[7,8,512]{2,1,0:T(8,128)S(1)} %copy-done, f32[7,8,128]{2,1,0:T(8,128)S(1)} %collective-permute-done.before, f32[7,8,128]{2,1,0:T(8,128)S(1)} %collective-permute-done.1.after, bf16[7,64,512]{2,1,0:T(8,128)(2,1)S(1)} %bitcast.16, s32[6,512]{1,0:T(8,128)S(1)} %copy-done.6, ...), custom_call_target="tpu_custom_call" | custom-call | flops 1000 | bytes 4000000 | tf_op jit(solution)/shard_map/window/pallas_call | solution.py:388
  29.4 0.0 all-to-all-done
  29.4 3.0 %collective-permute-start.2 = (f32[864,128]{1,0:T(8,128)S(1)}, f32[864,128]{1,0:T(8,128)S(1)}, u32[]{:S(2)}, u32[]{:S(2)}) collective-permute-start(f32[864,128]{1,0:T(8,128)S(1)} %bitcast.12), channel_id=1, source_target_pairs={{0,4},{4,0},{8,12},{12,8},{16,20},{20,16},{24,28},{28,24},{32,36},... | collective-permute-start | bytes 1327112 | tf_op jit(solution)/shard_map/ppermute | solution.py:408
  32.4 1.4 %collective-permute-done.2.other = f32[864,128]{1,0:T(8,128)S(1)} collective-permute-done((f32[864,128]{1,0:T(8,128)S(1)}, f32[864,128]{1,0:T(8,128)S(1)}, u32[]{:S(2)}, u32[]{:S(2)}) %collective-permute-start.2) | collective-permute-done | bytes 442400 | tf_op jit(solution)/shard_map/ppermute | solution.py:408
  33.8 0.0 copy-done.8
  33.8 0.5 %lookup.1.d0 = f32[32,256]{1,0:T(8,128)S(1)} custom-call(f32[864,128]{1,0:T(8,128)S(1)} %bitcast.13, f32[864,128]{1,0:T(8,128)S(1)} %collective-permute-done.2.other, s32[1,256]{1,0:T(1,128)S(1)} %bitcast.21, s32[1,256]{1,0:T(1,128)S(1)} %bitcast.23, f32[3,256]{1,0:T(4,128)S(1)} %copy-done.8, s32[1]{0:T(128)} %bitcast.8.core), custom_call_target="tpu_custom_call" | custom-call | flops 1000 | bytes 100000 | tf_op jit(solution)/shard_map/lookup/pallas_call | solution.py:409
  34.3 2.8 %collective-permute-start.5 = (f32[32,256]{1,0:T(8,128)S(1)}, f32[32,256]{1,0:T(8,128)S(1)}, u32[]{:S(2)}, u32[]{:S(2)}) collective-permute-start(f32[32,256]{1,0:T(8,128)S(1)} %lookup.1.d0), channel_id=1, source_target_pairs={{0,3},{1,0},{2,1},{3,2},{4,7},{5,4},{6,5},{7,6},{8,11},{9,8},{10,9... | collective-permute-start | bytes 98312 | tf_op jit(solution)/shard_map/ppermute | solution.py:413
  37.1 0.3 collective-permute-start.4
  37.5 0.7 %collective-permute-start.3 = (f32[32,256]{1,0:T(8,128)S(1)}, f32[32,256]{1,0:T(8,128)S(1)}, u32[]{:S(2)}, u32[]{:S(2)}) collective-permute-start(f32[32,256]{1,0:T(8,128)S(1)} %lookup.1.d0), channel_id=1, source_target_pairs={{0,1},{1,2},{2,3},{3,0},{4,5},{5,6},{6,7},{7,4},{8,9},{9,10},{10,1... | collective-permute-start | bytes 98312 | tf_op jit(solution)/shard_map/ppermute | solution.py:413
  38.2 0.7 %own.1 = (f32[512,32]{1,0:T(8,128)S(1)}, f32[512,48]{1,0:T(8,128)S(1)}) custom-call(f32[32,256]{1,0:T(8,128)S(1)} %lookup.1.d0, f32[3,512]{1,0:T(4,128)S(1)} %copy-done.7), custom_call_target="tpu_custom_call" | custom-call | flops 1000 | bytes 2000000 | tf_op jit(solution)/shard_map/own/pallas_call | solution.py:429
  38.9 0.0 copy-start.5
  38.9 1.2 %loads.1 = f32[3,7,128]{2,1,0:T(8,128)} custom-call(f32[864,128]{1,0:T(8,128)S(1)} %bitcast.14, f32[864,128]{1,0:T(8,128)S(1)} %collective-permute-done.2.other, f32[3,7,128]{2,1,0:T(8,128)S(1)} %get-tuple-element.19.part, s32[1]{0:T(128)} %bitcast.8.core), custom_call_target="tpu_custom_call" | custom-call | flops 1000 | bytes 2000000 | tf_op jit(solution)/shard_map/loads/pallas_call | solution.py:416
  40.0 0.0 collective-permute-done.5.d3
  40.0 1.4 %collective-permute-done.4.d2 = f32[32,256]{1,0:T(8,128)S(1)} collective-permute-done((f32[32,256]{1,0:T(8,128)S(1)}, f32[32,256]{1,0:T(8,128)S(1)}, u32[]{:S(2)}, u32[]{:S(2)}) %collective-permute-start.4) | collective-permute-done | bytes 32800 | tf_op jit(solution)/shard_map/ppermute | solution.py:413
  41.4 0.3 collective-permute-done.3.d1
  41.8 2.0 %final.1 = (f32[7,8,512]{2,1,0:T(8,128)}, f32[1,1]{1,0:T(1,128)}) custom-call(f32[32,256]{1,0:T(8,128)S(1)} %lookup.1.d0, f32[32,256]{1,0:T(8,128)S(1)} %collective-permute-done.3.d1, f32[32,256]{1,0:T(8,128)S(1)} %collective-permute-done.4.d2, f32[32,256]{1,0:T(8,128)S(1)} %collective-permute-done.5.d3, f32[512,32]{1,0:T(8,128)S(1)} %get-tuple-element.15.cols, ...), custom_call_target="tpu_custom_call" | custom-call | flops 1000 | bytes 100000 | tf_op jit(solution)/shard_map/final/pallas_call | solution.py:437
  (14 shorter events, 0.0 us)
Async XLA Ops:
  0.6 26.9 %copy-start.2 = (bf16[7,8,8,512]{3,2,1,0:T(8,128)(2,1)S(1)}, bf16[7,8,8,512]{3,2,1,0:T(8,128)(2,1)}, u32[]{:S(2)}) copy-start(bf16[7,8,8,512]{3,2,1,0:T(8,128)(2,1)} %param.18) | copy-start | bytes 1376260
  3.1 24.4 %copy-start.1 = (f32[3,128,3,128]{3,1,2,0:T(8,128)S(1)}, f32[3,128,3,128]{3,1,2,0:T(8,128)}, u32[]{:S(2)}) copy-start(f32[3,128,3,128]{3,1,2,0:T(8,128)} %param.29) | copy-start | bytes 1769476
  3.1 12.1 %copy-start = (f32[7,8,512]{2,1,0:T(8,128)S(1)}, f32[7,8,512]{2,1,0:T(8,128)}, u32[]{:S(2)}) copy-start(f32[7,8,512]{2,1,0:T(8,128)} %fluid.1) | copy-start | bytes 344068
  3.1 24.4 %copy-start.6 = (s32[6,512]{1,0:T(8,128)S(1)}, s32[6,512]{1,0:T(8,128)}, u32[]{:S(2)}) copy-start(s32[6,512]{1,0:T(8,128)} %nbr.1) | copy-start | bytes 36868
  3.1 24.4 %copy-start.11 = (f32[3,128]{1,0:T(4,128)S(1)}, f32[3,128]{1,0:T(4,128)}, u32[]{:S(2)}) copy-start(f32[3,128]{1,0:T(4,128)} %mass.1) | copy-start | bytes 4612
  3.2 26.3 %all-to-all-start = ((f32[32,1,3456]{2,1,0:T(1,128)}), f32[32,1,3456]{2,1,0:T(1,128)S(1)}, u32[]{:S(2)}, u32[]{:S(2)}) async-start(f32[32,1,3456]{2,1,0:T(1,128)} %bitcast.24), calls=%async_computation | async-start | bytes 884736 | tf_op jit(solution)/shard_map/all_to_all | solution.py:381
  15.2 12.4 %copy-start.3 = (f32[7,8,512]{2,1,0:T(8,128)S(1)}, f32[7,8,512]{2,1,0:T(8,128)}, u32[]{:S(2)}) copy-start(f32[7,8,512]{2,1,0:T(8,128)} %freq.1) | copy-start | bytes 344068
  15.2 12.4 %copy-start.4 = (f32[7,3,128]{2,0,1:T(8,128)S(1)}, f32[7,3,128]{2,0,1:T(8,128)}, u32[]{:S(2)}) copy-start(f32[7,3,128]{2,0,1:T(8,128)} %param.28) | copy-start | bytes 32260
  15.2 8.9 %collective-permute-start.1 = (f32[7,8,128]{2,1,0:T(8,128)S(1)}, f32[7,8,128]{2,1,0:T(8,128)S(1)}, u32[]{:S(2)}, u32[]{:S(2)}) collective-permute-start(f32[7,8,128]{2,1,0:T(8,128)S(1)} %get-tuple-element.21), channel_id=1, source_target_pairs={{1,0},{2,1},{3,2},{4,3},{5,4},{6,5},{7,6},{8,7},{9,8},{10,9},{11,1... | collective-permute-start | bytes 86024 | tf_op jit(solution)/shard_map/ppermute | solution.py:387
  20.8 6.7 %collective-permute-start = (f32[7,8,128]{2,1,0:T(8,128)S(1)}, f32[7,8,128]{2,1,0:T(8,128)S(1)}, u32[]{:S(2)}, u32[]{:S(2)}) collective-permute-start(f32[7,8,128]{2,1,0:T(8,128)S(1)} %get-tuple-element.22), channel_id=1, source_target_pairs={{0,1},{1,2},{2,3},{3,4},{4,5},{5,6},{6,7},{7,8},{8,9},{9,10},{10,1... | collective-permute-start | bytes 86024 | tf_op jit(solution)/shard_map/ppermute | solution.py:386
  29.4 4.4 %collective-permute-start.2 = (f32[864,128]{1,0:T(8,128)S(1)}, f32[864,128]{1,0:T(8,128)S(1)}, u32[]{:S(2)}, u32[]{:S(2)}) collective-permute-start(f32[864,128]{1,0:T(8,128)S(1)} %bitcast.12), channel_id=1, source_target_pairs={{0,4},{4,0},{8,12},{12,8},{16,20},{20,16},{24,28},{28,24},{32,36},... | collective-permute-start | bytes 1327112 | tf_op jit(solution)/shard_map/ppermute | solution.py:408
  32.4 1.4 %copy-start.8 = (f32[3,256]{1,0:T(4,128)S(1)}, f32[3,256]{1,0:T(4,128)}, u32[]{:S(2)}) copy-start(f32[3,256]{1,0:T(4,128)} %xyz.1) | copy-start | bytes 9220
  32.4 1.4 %copy-start.10 = (s32[256]{0:T(256)S(1)}, s32[256]{0:T(256)}, u32[]{:S(2)}) copy-start(s32[256]{0:T(256)} %param.25) | copy-start | bytes 3076
  32.4 1.4 %copy-start.9 = (s32[256,1]{0,1:T(1,128)S(1)}, s32[256,1]{0,1:T(1,128)}, u32[]{:S(2)}) copy-start(s32[256,1]{0,1:T(1,128)} %param.24) | copy-start | bytes 3076
  33.8 4.3 %copy-start.7 = (f32[3,512]{1,0:T(4,128)S(1)}, f32[3,512]{1,0:T(4,128)}, u32[]{:S(2)}) copy-start(f32[3,512]{1,0:T(4,128)} %cells.1) | copy-start | bytes 18436
  34.3 5.7 %collective-permute-start.5 = (f32[32,256]{1,0:T(8,128)S(1)}, f32[32,256]{1,0:T(8,128)S(1)}, u32[]{:S(2)}, u32[]{:S(2)}) collective-permute-start(f32[32,256]{1,0:T(8,128)S(1)} %lookup.1.d0), channel_id=1, source_target_pairs={{0,3},{1,0},{2,1},{3,2},{4,7},{5,4},{6,5},{7,6},{8,11},{9,8},{10,9... | collective-permute-start | bytes 98312 | tf_op jit(solution)/shard_map/ppermute | solution.py:413
  37.1 4.3 %collective-permute-start.4 = (f32[32,256]{1,0:T(8,128)S(1)}, f32[32,256]{1,0:T(8,128)S(1)}, u32[]{:S(2)}, u32[]{:S(2)}) collective-permute-start(f32[32,256]{1,0:T(8,128)S(1)} %lookup.1.d0), channel_id=1, source_target_pairs={{0,2},{1,3},{2,0},{3,1},{4,6},{5,7},{6,4},{7,5},{8,10},{9,11},{10,... | collective-permute-start | bytes 98312 | tf_op jit(solution)/shard_map/ppermute | solution.py:413
  37.5 4.3 %collective-permute-start.3 = (f32[32,256]{1,0:T(8,128)S(1)}, f32[32,256]{1,0:T(8,128)S(1)}, u32[]{:S(2)}, u32[]{:S(2)}) collective-permute-start(f32[32,256]{1,0:T(8,128)S(1)} %lookup.1.d0), channel_id=1, source_target_pairs={{0,1},{1,2},{2,3},{3,0},{4,5},{5,6},{6,7},{7,4},{8,9},{9,10},{10,1... | collective-permute-start | bytes 98312 | tf_op jit(solution)/shard_map/ppermute | solution.py:413
  38.9 2.9 %copy-start.5 = (f32[8,3,512]{2,0,1:T(8,128)S(1)}, f32[8,3,512]{2,0,1:T(8,128)}, u32[]{:S(2)}) copy-start(f32[8,3,512]{2,0,1:T(8,128)} %param.21) | copy-start | bytes 147460

commit v2 on v1

v2 whole, which is shorter than its diff:
```python
import functools

import jax
import jax.numpy as jnp
import numpy as np
from jax import lax
from jax.experimental import pallas as pl
from jax.experimental.pallas import tpu as pltpu
from jax.sharding import PartitionSpec as P

NT = 7
NV = 8
NF = 6
L = 128
CHIPS = 32
CAP = 16
ROWS = 27
F32 = jnp.float32
BF16 = jnp.bfloat16


def spectral_table(instances):
    positions = np.arange(instances)
    offset = positions[:, None] - positions[None, :]
    clipped = np.where(offset == 0, 1, offset)
    return np.where(
        offset == 0, 0.0, 0.5 * (-1.0) ** offset / np.sin(np.pi * clipped / instances)
    )


SPECTRAL = np.asarray(spectral_table(NT), np.float32)
SECOND = np.asarray(spectral_table(NT) @ spectral_table(NT), np.float32)


def iota(shape, axis):
    return lax.broadcasted_iota(jnp.int32, shape, axis)


def lanes_of(values, index):
    return jnp.take_along_axis(values, index, axis=1, mode="promise_in_bounds")


def thirds(values):
    high = values.astype(BF16)
    rest = values - high.astype(F32)
    middle = rest.astype(BF16)
    low = (rest - middle.astype(F32)).astype(BF16)
    return jnp.concatenate([high, middle, low], axis=0)


def dot_nt(a, b, precision=None):
    return lax.dot_general(
        a, b, (((1,), (1,)), ((), ())), precision=precision, preferred_element_type=F32
    )


def prep_kernel(*refs):
    far, out, tags, near = refs[:11], refs[11], refs[12], refs[13:24]
    pay, message, tag_rows, sems, out_sems = refs[24:]
    fluid, phase, cell, owner, node, proj, struct, xyz, nbr, mass, cells = near
    copies = [pltpu.make_async_copy(a, b, sems.at[i]) for i, (a, b) in enumerate(zip(far, near))]
    for i in (3, 4, 2, 0, 5, 6, 7, 8, 9, 10, 1):
        copies[i].start()
    pay[...] = jnp.zeros_like(pay)
    copies[3].wait()
    own = owner[...]
    hot = jnp.where(iota((64, 256), 0) == own, 1.0, 0.0)
    before = jnp.where(iota((256, 256), 0) < iota((256, 256), 1), 1.0, 0.0).astype(BF16)
    counts = jnp.dot(hot.astype(BF16), before, preferred_element_type=F32)
    rank = jnp.sum(hot * counts, axis=0, keepdims=True)
    slot = own * CAP + rank.astype(jnp.int32)
    slot_hot = jnp.where(iota((1024, 256), 0) == slot, 1.0, 0.0).astype(BF16)
    copies[4].wait()
    pay[pl.ds(27, 1), :] = (node[...] + 1).astype(F32)
    copies[2].wait()
    copies[6].wait()
    for p in range(CHIPS):
        for k in range(3):
            message[pl.ds(p * ROWS + k * NT, NT), :] = struct[k]
    copies[0].wait()
    copies[5].wait()
    for i in range(7, 11):
        copies[i].wait()
    tag_rows[...] = jnp.zeros_like(tag_rows)
    tag_rows[pl.ds(0, 1), :] = own.astype(F32)
    tag_rows[pl.ds(1, 1), :] = node[...].astype(F32)
    tag_rows[pl.ds(2, 3), :] = xyz[...]
    for k in range(3):
        tag_rows[pl.ds(32 + k * 8, NT), pl.ds(0, L)] = struct[k]
    tag_rows[pl.ds(8, 3), pl.ds(0, L)] = mass[...]
    for h in range(2):
        half = pl.ds(h * 256, 256)
        tag_rows[pl.ds(11 + 6 * h, 6), :] = nbr[:, half].astype(F32)
        tag_rows[pl.ds(23 + 3 * h, 3), :] = cells[:, half]
    sent = [pltpu.make_async_copy(tag_rows, tags, out_sems.at[4])]
    sent[0].start()
    for h in range(2):
        span = pl.ds(h * L, L)
        index = jnp.broadcast_to(cell[:, span], (8, L))
        lane, chunk = index & (L - 1), index >> 7
        for t in range(NT):
            got = lanes_of(fluid[t, :, pl.ds(0, L)], lane)
            for c in range(1, 4):
                got = jnp.where(chunk == c, lanes_of(fluid[t, :, pl.ds(c * L, L)], lane), got)
            for k in range(3):
                f = k * NT + t
                row = f // 6 * 8 + f % 6
                pay[pl.ds(row, 1), span] = jnp.sum(proj[k, :, span] * got, axis=0, keepdims=True)
    slotted = dot_nt(thirds(pay[...]), slot_hot)
    slotted = slotted[0:32] + slotted[32:64] + slotted[64:96]

    copies[1].wait()
    part = phase[0] * fluid[0]
    for t in range(1, NT):
        part = part + phase[t] * fluid[t]
    part = jnp.sum(part, axis=0, keepdims=True)
    part = part[:, 0:L] + part[:, L : 2 * L] + part[:, 2 * L : 3 * L] + part[:, 3 * L : 4 * L]
    part = part + pltpu.roll(part, 64, 1)
    part = part + pltpu.roll(part, 32, 1)
    is_phase = iota((8, L), 0) == 4
    place = iota((8, L), 1) >> 5
    for c in range(8):
        groups = [slotted[g * 8 : g * 8 + 8, c * L : c * L + L] for g in range(4)]
        groups[3] = jnp.where(is_phase, part, groups[3])
        turned = []
        for d in range(4):
            mixed = groups[d]
            for j in range(1, 4):
                mixed = jnp.where(place == j, groups[(j + d) % 4], mixed)
            turned.append(pltpu.roll(mixed, 32 * d, 1) if d else mixed)
        for j in range(4):
            packed = turned[(0 - j) % 4]
            for g in range(1, 4):
                packed = jnp.where(place == g, turned[(g - j) % 4], packed)
            message[pl.ds((c * 4 + j) * ROWS + 21, 6), :] = packed[0:6]
        if c % 2:
            span = pl.ds((c - 1) * 4 * ROWS, 8 * ROWS)
            copy = pltpu.make_async_copy(message.at[span], out.at[span], out_sems.at[c // 2])
            copy.start()
            sent.append(copy)
    for copy in sent:
        copy.wait()


def sides_kernel(fluid, tags, near, far):
    even = (lax.axis_index("cell") & 1) == 0
    for t in range(NT):
        first, last = fluid[t, :, pl.ds(0, L)], fluid[t, :, pl.ds(3 * L, L)]
        near[pl.ds(t * 8, 8), :] = jnp.where(even, last, first)
        far[t] = jnp.where(even, first, last)
    near[pl.ds(56, 8), :] = tags[pl.ds(0, 8), pl.ds(0, L)]
    near[pl.ds(64, 8), :] = tags[pl.ds(0, 8), pl.ds(L, L)]


def fold(level):
    for s in (4, 2, 1):
        half = len(level) // 2
        low = (iota((8, L), 0) & s) == 0
        level = [
            jnp.where(
                low,
                level[v] + pltpu.roll(level[v], 8 - s, 0),
                level[v + half] + pltpu.roll(level[v + half], s, 0),
            )
            for v in range(half)
        ]
    return level[0]


def gain(sums, jac, f, span, val):
    for vv in range(4):
        pair = jac[f, pl.ds(vv * 16, 16), span].astype(F32)
        for u in range(2):
            term = pair[u * 8 : u * 8 + 8] * val
            v = vv * 2 + u
            sums[v] = term if sums[v] is None else sums[v] + term


def window_kernel(
    fluid,
    near,
    jac,
    stiff,
    tags,
    omega_ref,
    dfreq_ref,
    flux,
    part,
    rate,
    cols,
    basis,
    near_basis,
    gathered,
    feats,
    rows,
    squared,
    rows2,
    squared2,
):
    even = (lax.axis_index("cell") & 1) == 0
    omega = omega_ref[...].reshape(1, 1)
    rate[...] = jnp.broadcast_to(dfreq_ref[...].reshape(1, 1), (8, L))
    for i in range(4):
        span = pl.ds(i * L, L)
        for f in range(NF):
            row = tags[pl.ds(11 + 6 * (i // 2) + f, 1), pl.ds(i % 2 * L, L)]
            off = jnp.broadcast_to(row, (8, L)).astype(jnp.int32)
            place = iota((8, L), 1) + L + off
            lane = place & (L - 1)
            which = jnp.where(off == 0, 3, place >> 7)
            for t in range(NT):
                got = jnp.zeros((8, L), F32)
                for q in range(3):
                    j = i + q
                    if j in (0, 5):
                        src = jnp.where(even == (j == 5), near[pl.ds(t * 8, 8), :], 0.0)
                    else:
                        src = fluid[t, :, pl.ds((j - 1) * L, L)]
                    got = jnp.where(which == q, lanes_of(src, lane), got)
                gathered[f, t] = got
        for t in range(NT):
            here = fluid[t, :, span]
            sums = [None] * 8
            for f in range(NF + 1):
                val = here if f == 0 else gathered[f - 1, t]
                gain(sums, jac, f, span, val)
            total = fold(sums)
            turn = None
            for s in range(NT):
                if s != t:
                    term = float(SPECTRAL[t, s]) * fluid[s, :, span]
                    turn = term if turn is None else turn + term
            flux[t, :, span] = total + omega * turn
    for k in range(3):
        acc = None
        for q in range(3):
            term = dot_nt(tags[pl.ds(32 + q * 8, NT), pl.ds(0, L)], stiff[k, q], lax.Precision.HIGHEST)
            acc = term if acc is None else acc + term
        for t in range(NT):
            turn = None
            for s in range(NT):
                term = float(SECOND[t, s]) * tags[pl.ds(32 + k * 8 + s, 1), pl.ds(0, L)]
                turn = term if turn is None else turn + term
            part[k, pl.ds(t, 1), :] = acc[t : t + 1] + omega * omega * tags[pl.ds(8 + k, 1), pl.ds(0, L)] * turn

    points = [
        jnp.concatenate([tags[pl.ds(23 + k, 1), :], tags[pl.ds(26 + k, 1), :]], axis=1)
        for k in range(3)
    ]
    features(points, 1.0, False, feats)
    turned = feats[...].T
    cols[...] = turned
    centres = [tags[pl.ds(2 + k, 1), :] for k in range(3)]
    basis_of(centres, turned.astype(BF16), rows, squared, basis)
    centres = [
        jnp.concatenate([near[pl.ds(58 + k, 1), :], near[pl.ds(66 + k, 1), :]], axis=1)
        for k in range(3)
    ]
    basis_of(centres, turned.astype(BF16), rows2, squared2, near_basis)


def edge_kernel(far, jac, tags, out):
    even = (lax.axis_index("cell") & 1) == 0
    at = pl.multiple_of(jnp.where(even, 0, 3 * L), L)
    want = jnp.where(even, 0, 2)
    places = []
    for f in range(NF):
        first, last = tags[pl.ds(11 + f, 1), pl.ds(0, L)], tags[pl.ds(17 + f, 1), pl.ds(L, L)]
        off = jnp.broadcast_to(jnp.where(even, first, last), (8, L)).astype(jnp.int32)
        places.append(iota((8, L), 1) + L + off)
    for t in range(NT):
        sums = [None] * 8
        for f in range(NF):
            got = lanes_of(far[t], places[f] & (L - 1))
            val = jnp.where((places[f] >> 7) == want, got, 0.0)
            gain(sums, jac, f + 1, pl.ds(at, L), val)
        out[t] = fold(sums)


def lookup_kernel(table, tags, other_tags, out, far):
    q = lax.axis_index("sec") & 1
    last = iota((8, L), 0) == 7
    total = table[pl.ds(25, 1), :]
    for p in range(1, CHIPS):
        total = total + table[pl.ds(p * ROWS + 25, 1), :]
    total = jnp.broadcast_to(total, (8, L))
    for other, (tag, to) in enumerate(((tags, out), (other_tags, far))):
        for h in range(2):
            span = pl.ds(h * L, L)
            own = jnp.broadcast_to(tag[pl.ds(0, 1), span], (8, L)).astype(jnp.int32)
            lane = jnp.broadcast_to(tag[pl.ds(1, 1), span], (8, L)).astype(jnp.int32)
            key = jnp.where((own & 1) == q, own >> 1, -1)
            found = [jnp.zeros((8, L), F32) for _ in range(3)]
            for p in range(CHIPS):
                hit = key == p
                for k in range(3):
                    values = table[pl.ds(p * ROWS + k * NT, 8), :]
                    found[k] = jnp.where(hit, lanes_of(values, lane), found[k])
            for k in range(3):
                extra = 0.0 if other else jnp.broadcast_to(tag[pl.ds(2 + k, 1), span], (8, L))
                to[pl.ds(h * 32 + k * 8, 8), :] = jnp.where(last, extra, found[k])
            to[pl.ds(h * 32 + 24, 8), :] = total
    for p in range(CHIPS):
        far[pl.ds(64 + p * 8, 8), :] = table[pl.ds(p * ROWS + 19, 8), :]


def node_sums(table, stride, base, dense):
    q = lax.axis_index("sec") & 1
    block = iota((8, L), 1) >> 4
    for c in range(4):
        shifted = []
        for i in range(8):
            values = table[pl.ds((c * 8 + i) * stride + base, 8), :]
            shifted.append(jnp.where(q == 1, pltpu.roll(values, L - 16, 1), values))
        for g in range(4):
            packed = None
            for i in range(8):
                turn = (16 * i - 32 * g) % L
                moved = pltpu.roll(shifted[i], turn, 1) if turn else shifted[i]
                packed = moved if packed is None else jnp.where(block == i, moved, packed)
            dense[pl.ds(g * 8, 8), pl.ds(c * L, L)] = packed
    tags = dense[pl.ds(29, 1), :].astype(jnp.int32)
    node_hot = jnp.where(iota((L, 512), 0) + 1 == tags, 1.0, 0.0).astype(BF16)
    loads = dot_nt(thirds(dense[...]), node_hot)
    return loads[0:32] + loads[32:64] + loads[64:96]


def own_loads_kernel(table, out, dense):
    out[...] = node_sums(table, ROWS, 19, dense)


def loads_kernel(other, sums, part, out, dense):
    loads = node_sums(other, 8, 64, dense) + sums[...]
    for k in range(3):
        for t in range(NT):
            f = k * NT + t
            row = f // 6 * 8 + f % 6 + 2
            out[k, pl.ds(t, 1), :] = part[k, pl.ds(t, 1), :] - loads[row : row + 1]


def parts_of(values):
    high = values.astype(BF16).astype(F32)
    rest = values - high
    middle = rest.astype(BF16).astype(F32)
    return high, middle, rest - middle


def features(xyz, scale, ones_first, out):
    at = 0
    square = None
    for point in xyz:
        square = point * point if square is None else square + point * point
        p = [scale * part for part in parts_of(point)]
        order = (0, 0, 1, 1, 0, 2) if ones_first else (0, 1, 0, 1, 2, 0)
        for i in order:
            out[pl.ds(at, 1), :] = p[i]
            at += 1
    one = jnp.ones_like(square)
    squares = list(parts_of(square))
    for row in [one] * 3 + squares if ones_first else squares + [one] * 3:
        out[pl.ds(at, 1), :] = row
        at += 1
    out[pl.ds(24, 8), :] = jnp.zeros((8, square.shape[1]), F32)


def basis_of(centres, cols, rows, squared, basis):
    features(centres, -2.0, True, rows)
    squared[...] = jnp.dot(cols, rows[...].astype(BF16), preferred_element_type=F32)
    for c in range(8):
        span = pl.ds(c * 64, 64)
        gap = jnp.maximum(squared[span, :], 1e-30)
        dist = gap * lax.rsqrt(gap)
        fall = jnp.maximum(1.0 - dist, 0.0)
        fall = fall * fall
        value = fall * fall * (4.0 * dist + 1.0)
        high = value.astype(BF16)
        basis[span, pl.ds(0, 256)] = high
        basis[span, pl.ds(256, 256)] = (value - high.astype(F32)).astype(BF16)


def halves(ref):
    return jnp.concatenate([ref[pl.ds(0, 24), :], ref[pl.ds(32, 24), :]], axis=1)


def moved_by(both, basis):
    high = both.astype(BF16).astype(F32)
    upper = jnp.concatenate([high, both - high], axis=0).astype(BF16)
    lower = jnp.concatenate([high, jnp.zeros_like(high)], axis=0).astype(BF16)
    return dot_nt(basis[...], jnp.concatenate([upper, lower], axis=1))


def block_of(ref, cols, rows, squared, basis):
    both = halves(ref)
    centres = [both[k * 8 + 7 : k * 8 + 8] for k in range(3)]
    basis_of(centres, cols[...].astype(BF16), rows, squared, basis)
    return moved_by(both, basis)


def first_kernel(d0, d2, cols, own_basis, out, rows, squared, basis):
    out[...] = moved_by(halves(d0), own_basis) + block_of(d2, cols, rows, squared, basis)


def block_kernel(ref, cols, moved, out, rows, squared, basis):
    out[...] = moved[...] + block_of(ref, cols, rows, squared, basis)


def final_kernel(
    d0, d1, d2, d3, near_basis, moved, sens, flux, freq, rate, edge, out, phase_out
):
    total = moved[...] + moved_by(halves(d1), near_basis)
    turned = total.T
    motion = turned[0:24] + turned[24:48]
    for t in range(NT):
        total = flux[t] + rate[pl.ds(0, 1), pl.ds(0, 1)] * freq[t]
        for k in range(3):
            total = total + sens[k] * motion[k * 8 + t : k * 8 + t + 1]
        out[t] = total
    even = (lax.axis_index("cell") & 1) == 0
    span = pl.ds(pl.multiple_of(jnp.where(even, 0, 3 * L), L), L)
    for t in range(NT):
        out[t, :, span] = out[t, :, span] + edge[t]
    row = pl.ds(24, 1), pl.ds(0, L)
    total = (d0[row] + d1[row]) + (d2[row] + d3[row])
    total = jnp.where(iota((1, L), 1) >= 96, total, 0.0)
    phase_out[0, 0] = jnp.sum(total)


VM = pl.BlockSpec(memory_space=pltpu.VMEM)
HBM = pl.BlockSpec(memory_space=pltpu.HBM)
SM = pl.BlockSpec(memory_space=pltpu.SMEM)


def kernel(body, name, ins, shapes, outs=None, types=None, scratch=(), size=100000, vmem=32):
    return pl.pallas_call(
        body,
        out_shape=[
            jax.ShapeDtypeStruct(s, t) for s, t in zip(shapes, types or [F32] * len(shapes))
        ],
        in_specs=ins,
        out_specs=outs or [VM] * len(shapes),
        scratch_shapes=list(scratch),
        name=name,
        compiler_params=pltpu.CompilerParams(vmem_limit_bytes=vmem * 1024 * 1024),
        cost_estimate=pl.CostEstimate(flops=1000, bytes_accessed=size, transcendentals=0),
    )


def on_device(
    fluid_delta,
    jacobian,
    face_nbr,
    freq_col,
    grid_sens,
    cell_xyz,
    surf_cell,
    surf_owner,
    surf_node,
    load_proj,
    surf_xyz,
    struct_delta,
    stiffness,
    mass,
    omega,
    freq_delta,
    phase_row,
):
    sections = lax.axis_size("sec")
    columns = lax.axis_size("cell")
    both = sections * columns
    struct = jnp.transpose(struct_delta, (1, 0, 2))
    stiff = jnp.transpose(stiffness, (0, 2, 1, 3))
    jac = jacobian.reshape(NF + 1, 64, 512)
    sens = jnp.transpose(grid_sens, (1, 0, 2))
    owner = surf_owner.reshape(1, 256)
    node = surf_node.reshape(1, 256)
    cell = surf_cell.reshape(1, 256)

    message, tags = kernel(
        prep_kernel,
        "prep",
        [HBM] * 11,
        [(CHIPS * ROWS, L), (56, 256)],
        outs=[HBM] * 2,
        scratch=[
            pltpu.VMEM((NT, NV, 512), F32),
            pltpu.VMEM((NT, NV, 512), F32),
            pltpu.VMEM((1, 256), jnp.int32),
            pltpu.VMEM((1, 256), jnp.int32),
            pltpu.VMEM((1, 256), jnp.int32),
            pltpu.VMEM((3, NV, 256), F32),
            pltpu.VMEM((3, NT, L), F32),
            pltpu.VMEM((3, 256), F32),
            pltpu.VMEM((NF, 512), jnp.int32),
            pltpu.VMEM((3, L), F32),
            pltpu.VMEM((3, 512), F32),
            pltpu.VMEM((32, 256), F32),
            pltpu.VMEM((CHIPS * ROWS, L), F32),
            pltpu.VMEM((56, 256), F32),
            pltpu.SemaphoreType.DMA((11,)),
            pltpu.SemaphoreType.DMA((5,)),
        ],
        vmem=60,
    )(
        fluid_delta,
        phase_row,
        cell,
        owner,
        node,
        load_proj,
        struct,
        surf_xyz,
        face_nbr,
        mass,
        cell_xyz,
    )
    groups = [[2 * i + c for i in range(sections // 2)] for c in range(2)]
    mine = lax.all_to_all(
        message.reshape(CHIPS, 1, ROWS * L), "sec", 0, 0, axis_index_groups=groups, tiled=True
    ).reshape(CHIPS * ROWS, L)
    swap = [(i, i ^ 1) for i in range(sections)]
    other_tags = lax.ppermute(tags, "sec", swap)
    pairs = [[(i, i ^ 1) for i in range(both)], [(i, ((i + 1) ^ 1) - 1) for i in range(1, both - 1)]]
    near_side, far_side = kernel(sides_kernel, "sides", [VM] * 2, [(72, L), (NT, NV, L)])(
        fluid_delta, tags
    )
    near_edge = lax.ppermute(near_side, ("sec", "cell"), pairs[0])
    far_edge = lax.ppermute(far_side, ("sec", "cell"), pairs[1])
    move = [
        pltpu.VMEM((32, 256), F32),
        pltpu.VMEM((512, 256), F32),
    ]
    flux, part, rate, cols, own_basis, near_basis = kernel(
        window_kernel,
        "window",
        [VM] * 7,
        [(NT, NV, 512), (3, NT, L), (8, L), (512, 32), (512, 512), (512, 512)],
        types=[F32] * 4 + [BF16] * 2,
        scratch=[pltpu.VMEM((NF, NT, 8, L), F32), pltpu.VMEM((32, 512), F32)] + move * 2,
        size=4 * 10**6,
    )(
        fluid_delta,
        near_edge,
        jac,
        stiff,
        tags,
        omega,
        freq_delta,
    )
    (edge,) = kernel(edge_kernel, "edge", [VM] * 3, [(NT, NV, L)])(far_edge, jac, tags)
    mine, flux, edge = lax.optimization_barrier((mine, flux, edge))
    near, far = kernel(lookup_kernel, "lookup", [VM] * 3, [(64, L), (320, L)])(
        mine, tags, other_tags
    )
    back = lax.ppermute(far, "sec", swap)
    (sums,) = kernel(
        own_loads_kernel, "own_loads", [VM], [(32, L)], scratch=[pltpu.VMEM((32, 512), F32)]
    )(mine)
    back, sums = lax.optimization_barrier((back, sums))
    disp = near + back[:64]
    d2, d3, d1 = (
        lax.ppermute(disp, "cell", [(i, i ^ k) for i in range(columns)]) for k in (2, 3, 1)
    )
    (struct_out,) = kernel(
        loads_kernel,
        "loads",
        [VM] * 3,
        [(3, NT, L)],
        scratch=[pltpu.VMEM((32, 512), F32)],
        size=2 * 10**6,
    )(back, sums, part)
    move.append(pltpu.VMEM((512, 512), BF16))
    struct_out, d2 = lax.optimization_barrier((struct_out, d2))
    (moved,) = kernel(
        first_kernel, "first", [VM] * 4, [(512, 48)], scratch=move, size=2 * 10**6
    )(disp, d2, cols, own_basis)
    (moved,) = kernel(
        block_kernel, "block", [VM] * 3, [(512, 48)], scratch=move, size=2 * 10**6
    )(d3, cols, moved)
    fluid_out, phase_out = kernel(
        final_kernel,
        "final",
        [VM] * 11,
        [(NT, NV, 512), (1, 1)],
        outs=[VM, SM],
    )(disp, d1, d2, d3, near_basis, moved, sens, flux, freq_col, rate, edge)
    return fluid_out, jnp.transpose(struct_out, (1, 0, 2)), phase_out.reshape(1)


def solution(mesh):
    split = ("sec", "cell")
    return jax.shard_map(
        on_device,
        mesh=mesh,
        in_specs=(
            P(None, None, split),
            P(None, None, None, split),
            P(None, split),
            P(None, None, split),
            P(None, None, split),
            P(None, split),
            P(split),
            P(split, None),
            P(split),
            P(None, None, split),
            P(None, split),
            P(None, None, split),
            P(None, None, None, split),
            P(None, split),
            P(),
            P(),
            P(None, None, split),
        ),
        out_specs=(P(None, None, split), P(None, None, split), P()),
        check_vma=False,
    )
```

time: 44.1 us -> 42.8 us (0.971)
  starting transfers between devices: 26.4 us -> 25.3 us
    ppermute x6 -> x7, waiting for transfers between devices: 6.54 us -> 3.41 us  [the longest x1 1.39 us: on_device(): far_edge = lax.ppermute(far_side, ('sec', 'cell'), pairs[1])]
    all_to_all x1, waiting for transfers between devices: 0.01 us -> 3.01 us  [on_device(): lax.all_to_all(message.reshape(CHIPS, 1, ROWS * L), 'sec', 0, 0, axis_ind...]
    ppermute x6 -> x7, starting transfers between devices: 14.3 us -> 13.3 us  [the longest x1 3.99 us: on_device(): far_edge = lax.ppermute(far_side, ('sec', 'cell'), pairs[1])]
    pallas_call x6 -> x10, Pallas kernels: 8.67 us -> 8.74 us  [the longest x1 2.55 us: on_device(): kernel(prep_kernel, 'prep', [HBM] * 11, [(CHIPS * ROWS, L), (56, 256)], o...]
  transfers between devices with their start and end apart: 7 -> 8, of which waited for: 4 -> 4; matrix products, arithmetic and copies ran while one was open for 0% -> 0% of each run, Pallas kernels for 8% -> 11%
where the time goes in v2:
time: 42.8 us; the launch traced here: 42.6 us
  starting transfers between devices  25.3 us (59%)
  Pallas kernels  8.74 us (20%)
  waiting for transfers between devices  6.42 us (15%)
  between operations  2.09 us (5%)
    all_to_all x1, starting transfers between devices, on_device(): lax.all_to_all(message.reshape(CHIPS, 1, ROWS * L), 'sec', 0, 0, axis_ind...  12 us
    ppermute x1, starting transfers between devices, on_device(): far_edge = lax.ppermute(far_side, ('sec', 'cell'), pairs[1])  3.99 us
    ppermute x3, starting transfers between devices, on_device(): lax.ppermute(disp, 'cell', [(i, i ^ k) for i in range(columns)])  3.69 us
    ppermute x1, starting transfers between devices, on_device(): back = lax.ppermute(far, 'sec', swap)  3.14 us
    all_to_all x1, waiting for transfers between devices, on_device(): lax.all_to_all(message.reshape(CHIPS, 1, ROWS * L), 'sec', 0, 0, axis_ind...  3.01 us
    pallas_call x1, Pallas kernels, on_device(): kernel(prep_kernel, 'prep', [HBM] * 11, [(CHIPS * ROWS, L), (56, 256)], o...  2.55 us
    pallas_call x1, Pallas kernels, on_device(): kernel(window_kernel, 'window', [VM] * 7, [(NT, NV, 512), (3, NT, L), (8,...  1.76 us
    ppermute x1, waiting for transfers between devices, on_device(): far_edge = lax.ppermute(far_side, ('sec', 'cell'), pairs[1])  1.39 us
  transfers between devices with their start and end apart: 8, of which 4 were waited for; matrix products, arithmetic and copies ran while one was open for 0% of the time, Pallas kernels for 11%

profile of v2, /device:TPU:1, one launch (start us, length us, event | category | flops | bytes accessed | tf_op | source)
XLA Modules:
  0.0 42.6 jit_solution(18324860403144733071)
XLA Ops:
  0.6 2.6 %prep.1 = (f32[864,128]{1,0:T(8,128)}, f32[56,256]{1,0:T(8,128)}) custom-call(f32[7,8,512]{2,1,0:T(8,128)} %fluid.3, f32[7,8,512]{2,1,0:T(8,128)} %refs_1_.1, s32[1,256]{1,0:T(1,128)} %bitcast.20, s32[1,256]{1,0:T(1,128)} %bitcast.21, s32[1,256]{1,0:T(1,128)} %bitcast.22, f32[3,8,256]{2,1,0:T(8,128)} %refs_5_.1, f32[3,7,128]{2,1,0:T(8,128)} %bitcast.18, ...), custom_call_target="tpu_custom_call" | custom-call | flops 1000 | bytes 100000 | tf_op jit(solution)/shard_map/prep/pallas_call | solution.py:478
  3.2 0.0 copy-start.2
  3.2 0.0 copy-start.1
  3.2 0.0 copy-start
  3.2 12.0 %all-to-all-start = ((f32[32,1,3456]{2,1,0:T(1,128)}), f32[32,1,3456]{2,1,0:T(1,128)S(1)}, u32[]{:S(2)}, u32[]{:S(2)}) async-start(f32[32,1,3456]{2,1,0:T(1,128)} %bitcast.17), calls=%async_computation | async-start | bytes 884736 | tf_op jit(solution)/shard_map/all_to_all | solution.py:517
  15.2 0.0 copy-start.3
  15.3 1.0 %collective-permute-start.2 = (f32[56,256]{1,0:T(8,128)S(1)}, f32[56,256]{1,0:T(8,128)S(1)}, u32[]{:S(2)}, u32[]{:S(2)}) collective-permute-start(f32[56,256]{1,0:T(8,128)S(1)} %copy-done.2), channel_id=1, source_target_pairs={{0,4},{4,0},{8,12},{12,8},{16,20},{20,16},{24,28},{28,24},{32,36},... | collective-permute-start | bytes 172040 | tf_op jit(solution)/shard_map/ppermute | solution.py:521
  16.3 1.4 %collective-permute-start = (f32[72,128]{1,0:T(8,128)S(1)}, f32[72,128]{1,0:T(8,128)S(1)}, u32[]{:S(2)}, u32[]{:S(2)}) collective-permute-start(f32[72,128]{1,0:T(8,128)S(1)} %get-tuple-element.26), channel_id=1, source_target_pairs={{0,1},{1,0},{2,3},{3,2},{4,5},{5,4},{6,7},{7,6},{8,9},{9,8},{10,11... | collective-permute-start | bytes 110600 | tf_op jit(solution)/shard_map/ppermute | solution.py:526
  17.7 4.0 %collective-permute-start.1 = (f32[7,8,128]{2,1,0:T(8,128)S(1)}, f32[7,8,128]{2,1,0:T(8,128)S(1)}, u32[]{:S(2)}, u32[]{:S(2)}) collective-permute-start(f32[7,8,128]{2,1,0:T(8,128)S(1)} %get-tuple-element.28), channel_id=1, source_target_pairs={{1,2},{2,1},{3,4},{4,3},{5,6},{6,5},{7,8},{8,7},{9,10},{10,9},{11,... | collective-permute-start | bytes 86024 | tf_op jit(solution)/shard_map/ppermute | solution.py:527
  23.0 1.4 %collective-permute-done.1.far = f32[7,8,128]{2,1,0:T(8,128)S(1)} collective-permute-done((f32[7,8,128]{2,1,0:T(8,128)S(1)}, f32[7,8,128]{2,1,0:T(8,128)S(1)}, u32[]{:S(2)}, u32[]{:S(2)}) %collective-permute-start.1) | collective-permute-done | bytes 28704 | tf_op jit(solution)/shard_map/ppermute | solution.py:527
  24.4 0.2 edge.1
  24.6 0.0 collective-permute-done.near
  24.6 0.0 copy-done.3
  24.6 1.8 %window.1 = (f32[7,8,512]{2,1,0:T(8,128)S(1)}, f32[3,7,128]{2,1,0:T(8,128)S(1)}, f32[8,128]{1,0:T(8,128)S(1)}, f32[512,32]{1,0:T(8,128)S(1)}, bf16[512,512]{1,0:...) custom-call(f32[7,8,512]{2,1,0:T(8,128)S(1)} %copy-done.1, f32[72,128]{1,0:T(8,128)S(1)} %collective-permute-done.near, ...), custom_call_target="tpu_custom_call" | custom-call | flops 1000 | bytes 4000000 | tf_op jit(solution)/shard_map/window/pallas_call | solution.py:532
  26.4 3.0 %all-to-all-done = f32[32,1,3456]{2,1,0:T(1,128)S(1)} async-done(((f32[32,1,3456]{2,1,0:T(1,128)}), f32[32,1,3456]{2,1,0:T(1,128)S(1)}, u32[]{:S(2)}, u32[]{:S(2)}) %all-to-all-start) | async-done | bytes 442400 | tf_op jit(solution)/shard_map/all_to_all | solution.py:517
  29.4 0.0 collective-permute-done.2.other_tags
  29.4 0.5 %lookup.1 = (f32[64,128]{1,0:T(8,128)S(1)}, f32[320,128]{1,0:T(8,128)S(1)}) custom-call(f32[864,128]{1,0:T(8,128)S(1)} %bitcast.11, f32[56,256]{1,0:T(8,128)S(1)} %copy-done.2, f32[56,256]{1,0:T(8,128)S(1)} %collective-permute-done.2.other_tags), custom_call_target="tpu_custom_call" | custom-call | flops 1000 | bytes 100000 | tf_op jit(solution)/shard_map/lookup/pallas_call | solution.py:551
  29.9 3.1 %collective-permute-start.3 = (f32[320,128]{1,0:T(8,128)S(1)}, f32[320,128]{1,0:T(8,128)S(1)}, u32[]{:S(2)}, u32[]{:S(2)}) collective-permute-start(f32[320,128]{1,0:T(8,128)S(1)} %get-tuple-element.31), channel_id=1, source_target_pairs={{0,4},{4,0},{8,12},{12,8},{16,20},{20,16},{24,28},{28,24},{32,36},... | collective-permute-start | bytes 491528 | tf_op jit(solution)/shard_map/ppermute | solution.py:554
  33.1 0.4 own_loads.1.sums
  33.4 0.7 %collective-permute-done.3.other = f32[320,128]{1,0:T(8,128)S(1)} collective-permute-done((f32[320,128]{1,0:T(8,128)S(1)}, f32[320,128]{1,0:T(8,128)S(1)}, u32[]{:S(2)}, u32[]{:S(2)}) %collective-permute-start.3) | collective-permute-done | bytes 163872 | tf_op jit(solution)/shard_map/ppermute | solution.py:554
  34.1 2.9 %collective-permute-start.5 = (f32[64,128]{1,0:T(8,128)S(1)}, f32[64,128]{1,0:T(8,128)S(1)}, u32[]{:S(2)}, u32[]{:S(2)}) collective-permute-start(f32[64,128]{1,0:T(8,128)S(1)} %slice_add_fusion.d0), channel_id=1, source_target_pairs={{0,2},{1,3},{2,0},{3,1},{4,6},{5,7},{6,4},{7,5},{8,10},{9,11},{10,... | collective-permute-start | bytes 98312 | tf_op jit(solution)/shard_map/ppermute | solution.py:561
  37.0 0.8 %collective-permute-start.6 = (f32[64,128]{1,0:T(8,128)S(1)}, f32[64,128]{1,0:T(8,128)S(1)}, u32[]{:S(2)}, u32[]{:S(2)}) collective-permute-start(f32[64,128]{1,0:T(8,128)S(1)} %slice_add_fusion.d0), channel_id=1, source_target_pairs={{0,3},{1,2},{2,1},{3,0},{4,7},{5,6},{6,5},{7,4},{8,11},{9,10},{10,... | collective-permute-start | bytes 98312 | tf_op jit(solution)/shard_map/ppermute | solution.py:561
  37.8 0.0 collective-permute-start.4
  37.8 1.0 %loads.1 = f32[3,7,128]{2,1,0:T(8,128)} custom-call(f32[320,128]{1,0:T(8,128)S(1)} %collective-permute-done.3.other, f32[32,128]{1,0:T(8,128)S(1)} %own_loads.1.sums, f32[3,7,128]{2,1,0:T(8,128)S(1)} %get-tuple-element.34.part), custom_call_target="tpu_custom_call" | custom-call | flops 1000 | bytes 2000000 | tf_op jit(solution)/shard_map/loads/pallas_call | solution.py:563
  38.8 0.0 collective-permute-done.5.d2
  38.8 0.8 %first.1.moved = f32[512,48]{1,0:T(8,128)S(1)} custom-call(f32[64,128]{1,0:T(8,128)S(1)} %slice_add_fusion.d0, f32[64,128]{1,0:T(8,128)S(1)} %collective-permute-done.5.d2, f32[512,32]{1,0:T(8,128)S(1)} %get-tuple-element.37.cols, bf16[512,512]{1,0:T(8,128)(2,1)S(1)} %get-tuple-element.38.own_basis), custom_call_target="tpu_custom_call" | custom-call | flops 1000 | bytes 2000000 | tf_op jit(solution)/shard_map/first/pallas_call | solution.py:573
  39.6 0.0 copy-start.4
  39.6 0.0 copy-start.5
  39.6 1.4 %collective-permute-done.6.ref.d3 = f32[64,128]{1,0:T(8,128)S(1)} collective-permute-done((f32[64,128]{1,0:T(8,128)S(1)}, f32[64,128]{1,0:T(8,128)S(1)}, u32[]{:S(2)}, u32[]{:S(2)}) %collective-permute-start.6) | collective-permute-done | bytes 32800 | tf_op jit(solution)/shard_map/ppermute | solution.py:561
  41.0 0.5 %block.1.moved = f32[512,48]{1,0:T(8,128)S(1)} custom-call(f32[64,128]{1,0:T(8,128)S(1)} %collective-permute-done.6.ref.d3, f32[512,32]{1,0:T(8,128)S(1)} %get-tuple-element.37.cols, f32[512,48]{1,0:T(8,128)S(1)} %first.1.moved), custom_call_target="tpu_custom_call" | custom-call | flops 1000 | bytes 2000000 | tf_op jit(solution)/shard_map/block/pallas_call | solution.py:576
  41.5 0.0 collective-permute-done.4.d1
  41.6 1.0 %final.1 = (f32[7,8,512]{2,1,0:T(8,128)}, f32[1,1]{1,0:T(1,128)}) custom-call(f32[64,128]{1,0:T(8,128)S(1)} %slice_add_fusion.d0, f32[64,128]{1,0:T(8,128)S(1)} %collective-permute-done.4.d1, f32[64,128]{1,0:T(8,128)S(1)} %collective-permute-done.5.d2, f32[64,128]{1,0:T(8,128)S(1)} %collective-permute-done.6.ref.d3, ...), custom_call_target="tpu_custom_call" | custom-call | flops 1000 | bytes 100000 | tf_op jit(solution)/shard_map/final/pallas_call | solution.py:579
  (7 shorter events, 0.0 us)
Async XLA Ops:
  3.2 12.1 %copy-start.2 = (f32[56,256]{1,0:T(8,128)S(1)}, f32[56,256]{1,0:T(8,128)}, u32[]{:S(2)}) copy-start(f32[56,256]{1,0:T(8,128)} %get-tuple-element.25.tags) | copy-start | bytes 172036
  3.2 13.1 %copy-start.1 = (f32[7,8,512]{2,1,0:T(8,128)S(1)}, f32[7,8,512]{2,1,0:T(8,128)}, u32[]{:S(2)}) copy-start(f32[7,8,512]{2,1,0:T(8,128)} %fluid.3) | copy-start | bytes 344068
  3.2 21.2 %copy-start = (bf16[7,8,8,512]{3,2,1,0:T(8,128)(2,1)S(1)}, bf16[7,8,8,512]{3,2,1,0:T(8,128)(2,1)}, u32[]{:S(2)}) copy-start(bf16[7,8,8,512]{3,2,1,0:T(8,128)(2,1)} %param.18) | copy-start | bytes 1376260
  3.2 26.2 %all-to-all-start = ((f32[32,1,3456]{2,1,0:T(1,128)}), f32[32,1,3456]{2,1,0:T(1,128)S(1)}, u32[]{:S(2)}, u32[]{:S(2)}) async-start(f32[32,1,3456]{2,1,0:T(1,128)} %bitcast.17), calls=%async_computation | async-start | bytes 884736 | tf_op jit(solution)/shard_map/all_to_all | solution.py:517
  15.2 9.4 %copy-start.3 = (f32[3,128,3,128]{3,1,2,0:T(8,128)S(1)}, f32[3,128,3,128]{3,1,2,0:T(8,128)}, u32[]{:S(2)}) copy-start(f32[3,128,3,128]{3,1,2,0:T(8,128)} %param.29) | copy-start | bytes 1769476
  15.3 14.2 %collective-permute-start.2 = (f32[56,256]{1,0:T(8,128)S(1)}, f32[56,256]{1,0:T(8,128)S(1)}, u32[]{:S(2)}, u32[]{:S(2)}) collective-permute-start(f32[56,256]{1,0:T(8,128)S(1)} %copy-done.2), channel_id=1, source_target_pairs={{0,4},{4,0},{8,12},{12,8},{16,20},{20,16},{24,28},{28,24},{32,36},... | collective-permute-start | bytes 172040 | tf_op jit(solution)/shard_map/ppermute | solution.py:521
  16.3 8.3 %collective-permute-start = (f32[72,128]{1,0:T(8,128)S(1)}, f32[72,128]{1,0:T(8,128)S(1)}, u32[]{:S(2)}, u32[]{:S(2)}) collective-permute-start(f32[72,128]{1,0:T(8,128)S(1)} %get-tuple-element.26), channel_id=1, source_target_pairs={{0,1},{1,0},{2,3},{3,2},{4,5},{5,4},{6,7},{7,6},{8,9},{9,8},{10,11... | collective-permute-start | bytes 110600 | tf_op jit(solution)/shard_map/ppermute | solution.py:526
  17.7 6.7 %collective-permute-start.1 = (f32[7,8,128]{2,1,0:T(8,128)S(1)}, f32[7,8,128]{2,1,0:T(8,128)S(1)}, u32[]{:S(2)}, u32[]{:S(2)}) collective-permute-start(f32[7,8,128]{2,1,0:T(8,128)S(1)} %get-tuple-element.28), channel_id=1, source_target_pairs={{1,2},{2,1},{3,4},{4,3},{5,6},{6,5},{7,8},{8,7},{9,10},{10,9},{11,... | collective-permute-start | bytes 86024 | tf_op jit(solution)/shard_map/ppermute | solution.py:527
  29.9 4.2 %collective-permute-start.3 = (f32[320,128]{1,0:T(8,128)S(1)}, f32[320,128]{1,0:T(8,128)S(1)}, u32[]{:S(2)}, u32[]{:S(2)}) collective-permute-start(f32[320,128]{1,0:T(8,128)S(1)} %get-tuple-element.31), channel_id=1, source_target_pairs={{0,4},{4,0},{8,12},{12,8},{16,20},{20,16},{24,28},{28,24},{32,36},... | collective-permute-start | bytes 491528 | tf_op jit(solution)/shard_map/ppermute | solution.py:554
  34.1 4.7 %collective-permute-start.5 = (f32[64,128]{1,0:T(8,128)S(1)}, f32[64,128]{1,0:T(8,128)S(1)}, u32[]{:S(2)}, u32[]{:S(2)}) collective-permute-start(f32[64,128]{1,0:T(8,128)S(1)} %slice_add_fusion.d0), channel_id=1, source_target_pairs={{0,2},{1,3},{2,0},{3,1},{4,6},{5,7},{6,4},{7,5},{8,10},{9,11},{10,... | collective-permute-start | bytes 98312 | tf_op jit(solution)/shard_map/ppermute | solution.py:561
  37.0 4.0 %collective-permute-start.6 = (f32[64,128]{1,0:T(8,128)S(1)}, f32[64,128]{1,0:T(8,128)S(1)}, u32[]{:S(2)}, u32[]{:S(2)}) collective-permute-start(f32[64,128]{1,0:T(8,128)S(1)} %slice_add_fusion.d0), channel_id=1, source_target_pairs={{0,3},{1,2},{2,1},{3,0},{4,7},{5,6},{6,5},{7,4},{8,11},{9,10},{10,... | collective-permute-start | bytes 98312 | tf_op jit(solution)/shard_map/ppermute | solution.py:561
  37.8 3.7 %collective-permute-start.4 = (f32[64,128]{1,0:T(8,128)S(1)}, f32[64,128]{1,0:T(8,128)S(1)}, u32[]{:S(2)}, u32[]{:S(2)}) collective-permute-start(f32[64,128]{1,0:T(8,128)S(1)} %slice_add_fusion.d0), channel_id=1, source_target_pairs={{0,1},{1,0},{2,3},{3,2},{4,5},{5,4},{6,7},{7,6},{8,9},{9,8},{10,11... | collective-permute-start | bytes 98312 | tf_op jit(solution)/shard_map/ppermute | solution.py:561
  39.6 1.9 %copy-start.4 = (f32[7,8,512]{2,1,0:T(8,128)S(1)}, f32[7,8,512]{2,1,0:T(8,128)}, u32[]{:S(2)}) copy-start(f32[7,8,512]{2,1,0:T(8,128)} %freq.1) | copy-start | bytes 344068
  39.6 1.9 %copy-start.5 = (f32[8,3,512]{2,0,1:T(8,128)S(1)}, f32[8,3,512]{2,0,1:T(8,128)}, u32[]{:S(2)}) copy-start(f32[8,3,512]{2,0,1:T(8,128)} %param.21) | copy-start | bytes 147460

commit v3 on v2

--- a/solution.py
+++ b/solution.py
@@ -15,6 +15,7 @@
 CHIPS = 32
 CAP = 16
 ROWS = 27
+RUNS = ((0, 0, 6, 2), (0, 6, 1, 10), (1, 0, 5, 11), (1, 5, 2, 18), (2, 0, 4, 20), (2, 4, 3, 26))
 F32 = jnp.float32
 BF16 = jnp.bfloat16
 
@@ -56,7 +57,8 @@
 
 def prep_kernel(*refs):
     far, out, tags, near = refs[:11], refs[11], refs[12], refs[13:24]
-    pay, message, tag_rows, sems, out_sems = refs[24:]
+    pay, message, sems, out_sems = refs[24:]
+    tag_rows, sent = tags, []
     fluid, phase, cell, owner, node, proj, struct, xyz, nbr, mass, cells = near
     copies = [pltpu.make_async_copy(a, b, sems.at[i]) for i, (a, b) in enumerate(zip(far, near))]
     for i in (3, 4, 2, 0, 5, 6, 7, 8, 9, 10, 1):
@@ -92,8 +94,6 @@
         half = pl.ds(h * 256, 256)
         tag_rows[pl.ds(11 + 6 * h, 6), :] = nbr[:, half].astype(F32)
         tag_rows[pl.ds(23 + 3 * h, 3), :] = cells[:, half]
-    sent = [pltpu.make_async_copy(tag_rows, tags, out_sems.at[4])]
-    sent[0].start()
     for h in range(2):
         span = pl.ds(h * L, L)
         index = jnp.broadcast_to(cell[:, span], (8, L))
@@ -142,14 +142,15 @@
         copy.wait()
 
 
-def sides_kernel(fluid, tags, near, far):
+def sides_kernel(fluid, tags, near, far, centres):
     even = (lax.axis_index("cell") & 1) == 0
     for t in range(NT):
         first, last = fluid[t, :, pl.ds(0, L)], fluid[t, :, pl.ds(3 * L, L)]
         near[pl.ds(t * 8, 8), :] = jnp.where(even, last, first)
         far[t] = jnp.where(even, first, last)
-    near[pl.ds(56, 8), :] = tags[pl.ds(0, 8), pl.ds(0, L)]
-    near[pl.ds(64, 8), :] = tags[pl.ds(0, 8), pl.ds(L, L)]
+    for h in range(2):
+        near[pl.ds(56 + 8 * h, 8), :] = tags[pl.ds(0, 8), pl.ds(h * L, L)]
+        centres[pl.ds(8 * h, 8), :] = tags[pl.ds(0, 8), pl.ds(h * L, L)]
 
 
 def fold(level):
@@ -179,27 +180,27 @@
 def window_kernel(
     fluid,
     near,
+    centres3,
     jac,
+    freq,
     stiff,
     tags,
     omega_ref,
     dfreq_ref,
     flux,
     part,
-    rate,
-    cols,
-    basis,
-    near_basis,
+    kept,
+    basis0,
+    basis1,
+    basis3,
     gathered,
     feats,
     rows,
     squared,
-    rows2,
-    squared2,
 ):
     even = (lax.axis_index("cell") & 1) == 0
     omega = omega_ref[...].reshape(1, 1)
-    rate[...] = jnp.broadcast_to(dfreq_ref[...].reshape(1, 1), (8, L))
+    dfreq = dfreq_ref[...].reshape(1, 1)
     for i in range(4):
         span = pl.ds(i * L, L)
         for f in range(NF):
@@ -230,7 +231,7 @@
                 if s != t:
                     term = float(SPECTRAL[t, s]) * fluid[s, :, span]
                     turn = term if turn is None else turn + term
-            flux[t, :, span] = total + omega * turn
+            flux[t, :, span] = total + omega * turn + dfreq * freq[t, :, span]
     for k in range(3):
         acc = None
         for q in range(3):
@@ -248,15 +249,20 @@
         for k in range(3)
     ]
     features(points, 1.0, False, feats)
-    turned = feats[...].T
-    cols[...] = turned
-    centres = [tags[pl.ds(2 + k, 1), :] for k in range(3)]
-    basis_of(centres, turned.astype(BF16), rows, squared, basis)
-    centres = [
-        jnp.concatenate([near[pl.ds(58 + k, 1), :], near[pl.ds(66 + k, 1), :]], axis=1)
-        for k in range(3)
-    ]
-    basis_of(centres, turned.astype(BF16), rows2, squared2, near_basis)
+    kept[...] = feats[...]
+    cols = feats[...].T.astype(BF16)
+    for n, basis in enumerate((basis0, basis1, basis3)):
+        if n == 0:
+            centres = [tags[pl.ds(2 + k, 1), :] for k in range(3)]
+        else:
+            ref, at = ((near, 56), (centres3, 0))[n - 1]
+            centres = [
+                jnp.concatenate(
+                    [ref[pl.ds(at + 2 + k, 1), :], ref[pl.ds(at + 10 + k, 1), :]], axis=1
+                )
+                for k in range(3)
+            ]
+        basis_of(centres, cols, rows.at[n], squared.at[n], basis)
 
 
 def edge_kernel(far, jac, tags, out):
@@ -331,11 +337,8 @@
 
 def loads_kernel(other, sums, part, out, dense):
     loads = node_sums(other, 8, 64, dense) + sums[...]
-    for k in range(3):
-        for t in range(NT):
-            f = k * NT + t
-            row = f // 6 * 8 + f % 6 + 2
-            out[k, pl.ds(t, 1), :] = part[k, pl.ds(t, 1), :] - loads[row : row + 1]
+    for k, t, size, row in RUNS:
+        out[k, pl.ds(t, size), :] = part[k, pl.ds(t, size), :] - loads[row : row + size]
 
 
 def parts_of(values):
@@ -389,35 +392,45 @@
     return dot_nt(basis[...], jnp.concatenate([upper, lower], axis=1))
 
 
-def block_of(ref, cols, rows, squared, basis):
+def own_kernel(d0, kept, basis, out, cols):
+    cols[...] = kept[...].T
+    out[...] = moved_by(halves(d0), basis)
+
+
+def block_kernel(ref, cols, moved, out, rows, squared, basis):
     both = halves(ref)
     centres = [both[k * 8 + 7 : k * 8 + 8] for k in range(3)]
     basis_of(centres, cols[...].astype(BF16), rows, squared, basis)
-    return moved_by(both, basis)
-
-
-def first_kernel(d0, d2, cols, own_basis, out, rows, squared, basis):
-    out[...] = moved_by(halves(d0), own_basis) + block_of(d2, cols, rows, squared, basis)
-
-
-def block_kernel(ref, cols, moved, out, rows, squared, basis):
-    out[...] = moved[...] + block_of(ref, cols, rows, squared, basis)
+    out[...] = moved[...] + moved_by(both, basis)
 
 
 def final_kernel(
-    d0, d1, d2, d3, near_basis, moved, sens, flux, freq, rate, edge, out, phase_out
+    d0,
+    d1,
+    d2,
+    d3,
+    near_basis,
+    third_basis,
+    moved,
+    sens,
+    flux,
+    edge,
+    struct,
+    out,
+    struct_out,
+    phase_out,
 ):
-    total = moved[...] + moved_by(halves(d1), near_basis)
+    struct_out[...] = struct[...]
+    even = (lax.axis_index("cell") & 1) == 0
+    span = pl.ds(pl.multiple_of(jnp.where(even, 0, 3 * L), L), L)
+    total = moved[...] + moved_by(halves(d3), third_basis) + moved_by(halves(d1), near_basis)
     turned = total.T
     motion = turned[0:24] + turned[24:48]
     for t in range(NT):
-        total = flux[t] + rate[pl.ds(0, 1), pl.ds(0, 1)] * freq[t]
+        total = flux[t]
         for k in range(3):
             total = total + sens[k] * motion[k * 8 + t : k * 8 + t + 1]
         out[t] = total
-    even = (lax.axis_index("cell") & 1) == 0
-    span = pl.ds(pl.multiple_of(jnp.where(even, 0, 3 * L), L), L)
-    for t in range(NT):
         out[t, :, span] = out[t, :, span] + edge[t]
     row = pl.ds(24, 1), pl.ds(0, L)
     total = (d0[row] + d1[row]) + (d2[row] + d3[row])
@@ -480,7 +493,7 @@
         "prep",
         [HBM] * 11,
         [(CHIPS * ROWS, L), (56, 256)],
-        outs=[HBM] * 2,
+        outs=[HBM, VM],
         scratch=[
             pltpu.VMEM((NT, NV, 512), F32),
             pltpu.VMEM((NT, NV, 512), F32),
@@ -495,23 +508,27 @@
             pltpu.VMEM((3, 512), F32),
             pltpu.VMEM((32, 256), F32),
             pltpu.VMEM((CHIPS * ROWS, L), F32),
-            pltpu.VMEM((56, 256), F32),
             pltpu.SemaphoreType.DMA((11,)),
-            pltpu.SemaphoreType.DMA((5,)),
+            pltpu.SemaphoreType.DMA((4,)),
         ],
-        vmem=60,
+        vmem=32,
     )(
-        fluid_delta,
-        phase_row,
-        cell,
-        owner,
-        node,
-        load_proj,
-        struct,
-        surf_xyz,
-        face_nbr,
-        mass,
-        cell_xyz,
+        *(
+            pltpu.with_memory_space_constraint(x, pltpu.HBM)
+            for x in (
+                fluid_delta,
+                phase_row,
+                cell,
+                owner,
+                node,
+                load_proj,
+                struct,
+                surf_xyz,
+                face_nbr,
+                mass,
+                cell_xyz,
+            )
+        )
     )
     groups = [[2 * i + c for i in range(sections // 2)] for c in range(2)]
     mine = lax.all_to_all(
@@ -520,34 +537,37 @@
     swap = [(i, i ^ 1) for i in range(sections)]
     other_tags = lax.ppermute(tags, "sec", swap)
     pairs = [[(i, i ^ 1) for i in range(both)], [(i, ((i + 1) ^ 1) - 1) for i in range(1, both - 1)]]
-    near_side, far_side = kernel(sides_kernel, "sides", [VM] * 2, [(72, L), (NT, NV, L)])(
-        fluid_delta, tags
-    )
+    near_side, far_side, centres = kernel(
+        sides_kernel, "sides", [VM] * 2, [(72, L), (NT, NV, L), (16, L)]
+    )(fluid_delta, tags)
+    centres3 = lax.ppermute(centres, "cell", [(i, i ^ 3) for i in range(columns)])
     near_edge = lax.ppermute(near_side, ("sec", "cell"), pairs[0])
     far_edge = lax.ppermute(far_side, ("sec", "cell"), pairs[1])
-    move = [
-        pltpu.VMEM((32, 256), F32),
-        pltpu.VMEM((512, 256), F32),
-    ]
-    flux, part, rate, cols, own_basis, near_basis = kernel(
+    flux, part, kept, *bases = kernel(
         window_kernel,
         "window",
-        [VM] * 7,
-        [(NT, NV, 512), (3, NT, L), (8, L), (512, 32), (512, 512), (512, 512)],
-        types=[F32] * 4 + [BF16] * 2,
-        scratch=[pltpu.VMEM((NF, NT, 8, L), F32), pltpu.VMEM((32, 512), F32)] + move * 2,
+        [VM] * 9,
+        [(NT, NV, 512), (3, NT, L), (32, 512)] + [(512, 512)] * 3,
+        types=[F32] * 3 + [BF16] * 3,
+        scratch=[
+            pltpu.VMEM((NF, NT, 8, L), F32),
+            pltpu.VMEM((32, 512), F32),
+            pltpu.VMEM((3, 32, 256), F32),
+            pltpu.VMEM((3, 512, 256), F32),
+        ],
         size=4 * 10**6,
     )(
         fluid_delta,
         near_edge,
+        centres3,
         jac,
+        freq_col,
         stiff,
         tags,
         omega,
         freq_delta,
     )
-    (edge,) = kernel(edge_kernel, "edge", [VM] * 3, [(NT, NV, L)])(far_edge, jac, tags)
-    mine, flux, edge = lax.optimization_barrier((mine, flux, edge))
+    mine, flux, far_edge = lax.optimization_barrier((mine, flux, far_edge))
     near, far = kernel(lookup_kernel, "lookup", [VM] * 3, [(64, L), (320, L)])(
         mine, tags, other_tags
     )
@@ -555,7 +575,8 @@
     (sums,) = kernel(
         own_loads_kernel, "own_loads", [VM], [(32, L)], scratch=[pltpu.VMEM((32, 512), F32)]
     )(mine)
-    back, sums = lax.optimization_barrier((back, sums))
+    (edge,) = kernel(edge_kernel, "edge", [VM] * 3, [(NT, NV, L)])(far_edge, jac, tags)
+    back, sums, edge = lax.optimization_barrier((back, sums, edge))
     disp = near + back[:64]
     d2, d3, d1 = (
         lax.ppermute(disp, "cell", [(i, i ^ k) for i in range(columns)]) for k in (2, 3, 1)
@@ -568,21 +589,29 @@
         scratch=[pltpu.VMEM((32, 512), F32)],
         size=2 * 10**6,
     )(back, sums, part)
-    move.append(pltpu.VMEM((512, 512), BF16))
-    struct_out, d2 = lax.optimization_barrier((struct_out, d2))
+    moved, cols = kernel(own_kernel, "own", [VM] * 3, [(512, 48), (512, 32)])(
+        disp, kept, bases[0]
+    )
+    struct_out, moved, d2 = lax.optimization_barrier((struct_out, moved, d2))
     (moved,) = kernel(
-        first_kernel, "first", [VM] * 4, [(512, 48)], scratch=move, size=2 * 10**6
-    )(disp, d2, cols, own_basis)
-    (moved,) = kernel(
-        block_kernel, "block", [VM] * 3, [(512, 48)], scratch=move, size=2 * 10**6
-    )(d3, cols, moved)
-    fluid_out, phase_out = kernel(
+        block_kernel,
+        "block",
+        [VM] * 3,
+        [(512, 48)],
+        scratch=[
+            pltpu.VMEM((32, 256), F32),
+            pltpu.VMEM((512, 256), F32),
+            pltpu.VMEM((512, 512), BF16),
+        ],
+        size=10**6,
+    )(d2, cols, moved)
+    fluid_out, struct_out, phase_out = kernel(
         final_kernel,
         "final",
         [VM] * 11,
-        [(NT, NV, 512), (1, 1)],
-        outs=[VM, SM],
-    )(disp, d1, d2, d3, near_basis, moved, sens, flux, freq_col, rate, edge)
+        [(NT, NV, 512), (3, NT, L), (1, 1)],
+        outs=[VM, VM, SM],
+    )(disp, d1, d2, d3, bases[1], bases[2], moved, sens, flux, edge, struct_out)
     return fluid_out, jnp.transpose(struct_out, (1, 0, 2)), phase_out.reshape(1)
 
 

time: 42.8 us -> 42.5 us (level)
  starting transfers between devices: 25.3 us -> 27.3 us
  waiting for transfers between devices: 6.42 us -> 4.67 us
  Pallas kernels: 8.74 us -> 8.08 us
    ppermute x0 -> x1, starting transfers between devices: none -> 2.09 us  [on_device(): lax.ppermute(centres, 'cell', [(i, i ^ 3) for i in range(columns)])]
    all_to_all x1, waiting for transfers between devices: 3.01 us -> 1.59 us  [on_device(): lax.all_to_all(message.reshape(CHIPS, 1, ROWS * L), 'sec', 0, 0, axis_ind...]
    ppermute x1, waiting for transfers between devices: 1.39 us -> 0.01 us  [on_device(): far_edge = lax.ppermute(far_side, ('sec', 'cell'), pairs[1])]
    ppermute x0 -> x1, waiting for transfers between devices: none -> 0.7 us  [on_device(): lax.ppermute(centres, 'cell', [(i, i ^ 3) for i in range(columns)])]
    pallas_call x1, Pallas kernels: 1.01 us -> 0.4 us  [on_device(): kernel(loads_kernel, 'loads', [VM] * 3, [(3, NT, L)], scratch=[pltpu.VMEM...]
    ppermute x3, waiting for transfers between devices: 1.36 us -> 1.97 us  [on_device(): lax.ppermute(disp, 'cell', [(i, i ^ k) for i in range(columns)])]
  transfers between devices with their start and end apart: 8 -> 9, of which waited for: 4 -> 4; matrix products, arithmetic and copies ran while one was open for 0% -> 0% of each run, Pallas kernels for 11% -> 9%
where the time goes in v3:
time: 42.5 us; the launch traced here: 42.2 us
  starting transfers between devices  27.3 us (64%)
  Pallas kernels  8.08 us (19%)
  waiting for transfers between devices  4.67 us (11%)
  between operations  2.07 us (5%)
    all_to_all x1, starting transfers between devices, on_device(): lax.all_to_all(message.reshape(CHIPS, 1, ROWS * L), 'sec', 0, 0, axis_ind...  12 us
    ppermute x1, starting transfers between devices, on_device(): far_edge = lax.ppermute(far_side, ('sec', 'cell'), pairs[1])  3.99 us
    ppermute x3, starting transfers between devices, on_device(): lax.ppermute(disp, 'cell', [(i, i ^ k) for i in range(columns)])  3.69 us
    ppermute x1, starting transfers between devices, on_device(): back = lax.ppermute(far, 'sec', swap)  3.14 us
    pallas_call x1, Pallas kernels, on_device(): kernel(prep_kernel, 'prep', [HBM] * 11, [(CHIPS * ROWS, L), (56, 256)], o...  2.62 us
    ppermute x1, starting transfers between devices, on_device(): lax.ppermute(centres, 'cell', [(i, i ^ 3) for i in range(columns)])  2.09 us
    pallas_call x1, Pallas kernels, on_device(): kernel(window_kernel, 'window', [VM] * 9, [(NT, NV, 512), (3, NT, L), (32...  2.01 us
    ppermute x3, waiting for transfers between devices, on_device(): lax.ppermute(disp, 'cell', [(i, i ^ k) for i in range(columns)])  1.97 us
  transfers between devices with their start and end apart: 9, of which 4 were waited for; matrix products, arithmetic and copies ran while one was open for 0% of the time, Pallas kernels for 9%

profile of v3, /device:TPU:1, one launch (start us, length us, event | category | flops | bytes accessed | tf_op | source)
XLA Modules:
  0.0 42.2 jit_solution(14543428044484547847)
XLA Ops:
  0.6 0.0 copy-start.2
  0.6 2.6 %prep.1 = (f32[864,128]{1,0:T(8,128)}, f32[56,256]{1,0:T(8,128)S(1)}) custom-call(f32[7,8,512]{2,1,0:T(8,128)} %fluid.3, f32[7,8,512]{2,1,0:T(8,128)} %refs_1_.1, s32[1,256]{1,0:T(1,128)} %bitcast.18, s32[1,256]{1,0:T(1,128)} %bitcast.19, s32[1,256]{1,0:T(1,128)} %bitcast.20, f32[3,8,256]{2,1,0:T(8,128)} %refs_5_.1, f32[3,7,128]{2,1,0:T(8,128)} %bitcast.17, ...), custom_call_target="tpu_custom_call" | custom-call | flops 1000 | bytes 100000 | tf_op jit(solution)/shard_map/prep/pallas_call | solution.py:491
  3.3 0.0 copy-start.1
  3.3 0.0 copy-start
  3.3 12.0 %all-to-all-start = ((f32[32,1,3456]{2,1,0:T(1,128)}), f32[32,1,3456]{2,1,0:T(1,128)S(1)}, u32[]{:S(2)}, u32[]{:S(2)}) async-start(f32[32,1,3456]{2,1,0:T(1,128)} %bitcast.4), calls=%async_computation | async-start | bytes 884736 | tf_op jit(solution)/shard_map/all_to_all | solution.py:534
  15.3 0.0 copy-start.3
  15.3 1.0 %collective-permute-start.3 = (f32[56,256]{1,0:T(8,128)S(1)}, f32[56,256]{1,0:T(8,128)S(1)}, u32[]{:S(2)}, u32[]{:S(2)}) collective-permute-start(f32[56,256]{1,0:T(8,128)S(1)} %get-tuple-element.31.tags), channel_id=1, source_target_pairs={{0,4},{4,0},{8,12},{12,8},{16,20},{20,16},{24,28},{28,24},{32,36},... | collective-permute-start | bytes 172040 | tf_op jit(solution)/shard_map/ppermute | solution.py:538
  16.4 1.4 %collective-permute-start = (f32[72,128]{1,0:T(8,128)S(1)}, f32[72,128]{1,0:T(8,128)S(1)}, u32[]{:S(2)}, u32[]{:S(2)}) collective-permute-start(f32[72,128]{1,0:T(8,128)S(1)} %get-tuple-element.32), channel_id=1, source_target_pairs={{0,1},{1,0},{2,3},{3,2},{4,5},{5,4},{6,7},{7,6},{8,9},{9,8},{10,11... | collective-permute-start | bytes 110600 | tf_op jit(solution)/shard_map/ppermute | solution.py:544
  17.8 4.0 %collective-permute-start.2 = (f32[7,8,128]{2,1,0:T(8,128)S(1)}, f32[7,8,128]{2,1,0:T(8,128)S(1)}, u32[]{:S(2)}, u32[]{:S(2)}) collective-permute-start(f32[7,8,128]{2,1,0:T(8,128)S(1)} %get-tuple-element.35), channel_id=1, source_target_pairs={{1,2},{2,1},{3,4},{4,3},{5,6},{6,5},{7,8},{8,7},{9,10},{10,9},{11,... | collective-permute-start | bytes 86024 | tf_op jit(solution)/shard_map/ppermute | solution.py:545
  21.8 2.1 %collective-permute-start.1 = (f32[16,128]{1,0:T(8,128)S(1)}, f32[16,128]{1,0:T(8,128)S(1)}, u32[]{:S(2)}, u32[]{:S(2)}) collective-permute-start(f32[16,128]{1,0:T(8,128)S(1)} %get-tuple-element.33), channel_id=1, source_target_pairs={{0,3},{1,2},{2,1},{3,0},{4,7},{5,6},{6,5},{7,4},{8,11},{9,10},{10,... | collective-permute-start | bytes 24584 | tf_op jit(solution)/shard_map/ppermute | solution.py:543
  25.2 0.7 %collective-permute-done.1.centres3 = f32[16,128]{1,0:T(8,128)S(1)} collective-permute-done((f32[16,128]{1,0:T(8,128)S(1)}, f32[16,128]{1,0:T(8,128)S(1)}, u32[]{:S(2)}, u32[]{:S(2)}) %collective-permute-start.1) | collective-permute-done | bytes 8224 | tf_op jit(solution)/shard_map/ppermute | solution.py:543
  25.9 0.0 collective-permute-done.near
  25.9 2.0 %window.1 = (f32[7,8,512]{2,1,0:T(8,128)S(1)}, f32[3,7,128]{2,1,0:T(8,128)S(1)}, f32[32,512]{1,0:T(8,128)S(1)}, bf16[512,512]{1,0:T(8,128)(2,1)S(1)}, bf16[512,5...) custom-call(f32[7,8,512]{2,1,0:T(8,128)S(1)} %copy-done.1, f32[72,128]{1,0:T(8,128)S(1)} %collective-permute-done.near, ...), custom_call_target="tpu_custom_call" | custom-call | flops 1000 | bytes 4000000 | tf_op jit(solution)/shard_map/window/pallas_call | solution.py:546
  27.9 0.0 collective-permute-done.2.far
  27.9 1.6 %all-to-all-done = f32[32,1,3456]{2,1,0:T(1,128)S(1)} async-done(((f32[32,1,3456]{2,1,0:T(1,128)}), f32[32,1,3456]{2,1,0:T(1,128)S(1)}, u32[]{:S(2)}, u32[]{:S(2)}) %all-to-all-start) | async-done | bytes 442400 | tf_op jit(solution)/shard_map/all_to_all | solution.py:534
  29.5 0.0 collective-permute-done.3.other_tags
  29.5 0.5 %lookup.1 = (f32[64,128]{1,0:T(8,128)S(1)}, f32[320,128]{1,0:T(8,128)S(1)}) custom-call(f32[864,128]{1,0:T(8,128)S(1)} %bitcast.11, f32[56,256]{1,0:T(8,128)S(1)} %get-tuple-element.31.tags, f32[56,256]{1,0:T(8,128)S(1)} %collective-permute-done.3.other_tags), custom_call_target="tpu_custom_call" | custom-call | flops 1000 | bytes 100000 | tf_op jit(solution)/shard_map/lookup/pallas_call | solution.py:571
  30.0 3.1 %collective-permute-start.4 = (f32[320,128]{1,0:T(8,128)S(1)}, f32[320,128]{1,0:T(8,128)S(1)}, u32[]{:S(2)}, u32[]{:S(2)}) collective-permute-start(f32[320,128]{1,0:T(8,128)S(1)} %get-tuple-element.38), channel_id=1, source_target_pairs={{0,4},{4,0},{8,12},{12,8},{16,20},{20,16},{24,28},{28,24},{32,36},... | collective-permute-start | bytes 491528 | tf_op jit(solution)/shard_map/ppermute | solution.py:574
  33.1 0.4 own_loads.1.sums
  33.5 0.2 edge.1
  33.8 0.4 collective-permute-done.4.other
  34.2 2.9 %collective-permute-start.6 = (f32[64,128]{1,0:T(8,128)S(1)}, f32[64,128]{1,0:T(8,128)S(1)}, u32[]{:S(2)}, u32[]{:S(2)}) collective-permute-start(f32[64,128]{1,0:T(8,128)S(1)} %slice_add_fusion.d0), channel_id=1, source_target_pairs={{0,2},{1,3},{2,0},{3,1},{4,6},{5,7},{6,4},{7,5},{8,10},{9,11},{10,... | collective-permute-start | bytes 98312 | tf_op jit(solution)/shard_map/ppermute | solution.py:582
  37.1 0.8 %collective-permute-start.7 = (f32[64,128]{1,0:T(8,128)S(1)}, f32[64,128]{1,0:T(8,128)S(1)}, u32[]{:S(2)}, u32[]{:S(2)}) collective-permute-start(f32[64,128]{1,0:T(8,128)S(1)} %slice_add_fusion.d0), channel_id=1, source_target_pairs={{0,3},{1,2},{2,1},{3,0},{4,7},{5,6},{6,5},{7,4},{8,11},{9,10},{10,... | collective-permute-start | bytes 98312 | tf_op jit(solution)/shard_map/ppermute | solution.py:582
  37.8 0.0 collective-permute-start.5
  37.9 0.3 own.1
  38.1 0.4 loads.1.struct
  38.5 0.0 collective-permute-done.6.ref.d2
  38.5 0.0 copy-start.4
  38.5 0.5 %block.1.moved = f32[512,48]{1,0:T(8,128)S(1)} custom-call(f32[64,128]{1,0:T(8,128)S(1)} %collective-permute-done.6.ref.d2, f32[512,32]{1,0:T(8,128)S(1)} %get-tuple-element.49.cols, f32[512,48]{1,0:T(8,128)S(1)} %get-tuple-element.50.moved), custom_call_target="tpu_custom_call" | custom-call | flops 1000 | bytes 1000000 | tf_op jit(solution)/shard_map/block/pallas_call | solution.py:596
  39.1 2.0 %collective-permute-done.7.d3 = f32[64,128]{1,0:T(8,128)S(1)} collective-permute-done((f32[64,128]{1,0:T(8,128)S(1)}, f32[64,128]{1,0:T(8,128)S(1)}, u32[]{:S(2)}, u32[]{:S(2)}) %collective-permute-start.7) | collective-permute-done | bytes 32800 | tf_op jit(solution)/shard_map/ppermute | solution.py:582
  41.0 0.0 collective-permute-done.5.d1
  41.1 1.1 %final.1 = (f32[7,8,512]{2,1,0:T(8,128)}, f32[3,7,128]{2,1,0:T(8,128)}, f32[1,1]{1,0:T(1,128)}) custom-call(f32[64,128]{1,0:T(8,128)S(1)} %slice_add_fusion.d0, f32[64,128]{1,0:T(8,128)S(1)} %collective-permute-done.5.d1, f32[64,128]{1,0:T(8,128)S(1)} %collective-permute-done.6.ref.d2, f32[64,128]{1,0:T(8,128)S(1)} %collective-permute-done.7.d3, ...), custom_call_target="tpu_custom_call" | custom-call | flops 1000 | bytes 100000 | tf_op jit(solution)/shard_map/final/pallas_call | solution.py:608
  (7 shorter events, 0.0 us)
Async XLA Ops:
  0.6 25.2 %copy-start.2 = (f32[3,128,3,128]{3,1,2,0:T(8,128)S(1)}, f32[3,128,3,128]{3,1,2,0:T(8,128)}, u32[]{:S(2)}) copy-start(f32[3,128,3,128]{3,1,2,0:T(8,128)} %param.29) | copy-start | bytes 1769476
  3.3 13.1 %copy-start.1 = (f32[7,8,512]{2,1,0:T(8,128)S(1)}, f32[7,8,512]{2,1,0:T(8,128)}, u32[]{:S(2)}) copy-start(f32[7,8,512]{2,1,0:T(8,128)} %fluid.3) | copy-start | bytes 344068
  3.3 22.6 %copy-start = (bf16[7,8,8,512]{3,2,1,0:T(8,128)(2,1)S(1)}, bf16[7,8,8,512]{3,2,1,0:T(8,128)(2,1)}, u32[]{:S(2)}) copy-start(bf16[7,8,8,512]{3,2,1,0:T(8,128)(2,1)} %param.18) | copy-start | bytes 1376260
  3.3 26.2 %all-to-all-start = ((f32[32,1,3456]{2,1,0:T(1,128)}), f32[32,1,3456]{2,1,0:T(1,128)S(1)}, u32[]{:S(2)}, u32[]{:S(2)}) async-start(f32[32,1,3456]{2,1,0:T(1,128)} %bitcast.4), calls=%async_computation | async-start | bytes 884736 | tf_op jit(solution)/shard_map/all_to_all | solution.py:534
  15.3 10.6 %copy-start.3 = (f32[7,8,512]{2,1,0:T(8,128)S(1)}, f32[7,8,512]{2,1,0:T(8,128)}, u32[]{:S(2)}) copy-start(f32[7,8,512]{2,1,0:T(8,128)} %freq.1) | copy-start | bytes 344068
  15.3 14.2 %collective-permute-start.3 = (f32[56,256]{1,0:T(8,128)S(1)}, f32[56,256]{1,0:T(8,128)S(1)}, u32[]{:S(2)}, u32[]{:S(2)}) collective-permute-start(f32[56,256]{1,0:T(8,128)S(1)} %get-tuple-element.31.tags), channel_id=1, source_target_pairs={{0,4},{4,0},{8,12},{12,8},{16,20},{20,16},{24,28},{28,24},{32,36},... | collective-permute-start | bytes 172040 | tf_op jit(solution)/shard_map/ppermute | solution.py:538
  16.4 9.5 %collective-permute-start = (f32[72,128]{1,0:T(8,128)S(1)}, f32[72,128]{1,0:T(8,128)S(1)}, u32[]{:S(2)}, u32[]{:S(2)}) collective-permute-start(f32[72,128]{1,0:T(8,128)S(1)} %get-tuple-element.32), channel_id=1, source_target_pairs={{0,1},{1,0},{2,3},{3,2},{4,5},{5,4},{6,7},{7,6},{8,9},{9,8},{10,11... | collective-permute-start | bytes 110600 | tf_op jit(solution)/shard_map/ppermute | solution.py:544
  17.8 10.1 %collective-permute-start.2 = (f32[7,8,128]{2,1,0:T(8,128)S(1)}, f32[7,8,128]{2,1,0:T(8,128)S(1)}, u32[]{:S(2)}, u32[]{:S(2)}) collective-permute-start(f32[7,8,128]{2,1,0:T(8,128)S(1)} %get-tuple-element.35), channel_id=1, source_target_pairs={{1,2},{2,1},{3,4},{4,3},{5,6},{6,5},{7,8},{8,7},{9,10},{10,9},{11,... | collective-permute-start | bytes 86024 | tf_op jit(solution)/shard_map/ppermute | solution.py:545
  21.8 4.1 %collective-permute-start.1 = (f32[16,128]{1,0:T(8,128)S(1)}, f32[16,128]{1,0:T(8,128)S(1)}, u32[]{:S(2)}, u32[]{:S(2)}) collective-permute-start(f32[16,128]{1,0:T(8,128)S(1)} %get-tuple-element.33), channel_id=1, source_target_pairs={{0,3},{1,2},{2,1},{3,0},{4,7},{5,6},{6,5},{7,4},{8,11},{9,10},{10,... | collective-permute-start | bytes 24584 | tf_op jit(solution)/shard_map/ppermute | solution.py:543
  30.0 4.2 %collective-permute-start.4 = (f32[320,128]{1,0:T(8,128)S(1)}, f32[320,128]{1,0:T(8,128)S(1)}, u32[]{:S(2)}, u32[]{:S(2)}) collective-permute-start(f32[320,128]{1,0:T(8,128)S(1)} %get-tuple-element.38), channel_id=1, source_target_pairs={{0,4},{4,0},{8,12},{12,8},{16,20},{20,16},{24,28},{28,24},{32,36},... | collective-permute-start | bytes 491528 | tf_op jit(solution)/shard_map/ppermute | solution.py:574
  34.2 4.4 %collective-permute-start.6 = (f32[64,128]{1,0:T(8,128)S(1)}, f32[64,128]{1,0:T(8,128)S(1)}, u32[]{:S(2)}, u32[]{:S(2)}) collective-permute-start(f32[64,128]{1,0:T(8,128)S(1)} %slice_add_fusion.d0), channel_id=1, source_target_pairs={{0,2},{1,3},{2,0},{3,1},{4,6},{5,7},{6,4},{7,5},{8,10},{9,11},{10,... | collective-permute-start | bytes 98312 | tf_op jit(solution)/shard_map/ppermute | solution.py:582
  37.1 4.0 %collective-permute-start.7 = (f32[64,128]{1,0:T(8,128)S(1)}, f32[64,128]{1,0:T(8,128)S(1)}, u32[]{:S(2)}, u32[]{:S(2)}) collective-permute-start(f32[64,128]{1,0:T(8,128)S(1)} %slice_add_fusion.d0), channel_id=1, source_target_pairs={{0,3},{1,2},{2,1},{3,0},{4,7},{5,6},{6,5},{7,4},{8,11},{9,10},{10,... | collective-permute-start | bytes 98312 | tf_op jit(solution)/shard_map/ppermute | solution.py:582
  37.8 3.2 %collective-permute-start.5 = (f32[64,128]{1,0:T(8,128)S(1)}, f32[64,128]{1,0:T(8,128)S(1)}, u32[]{:S(2)}, u32[]{:S(2)}) collective-permute-start(f32[64,128]{1,0:T(8,128)S(1)} %slice_add_fusion.d0), channel_id=1, source_target_pairs={{0,1},{1,0},{2,3},{3,2},{4,5},{5,4},{6,7},{7,6},{8,9},{9,8},{10,11... | collective-permute-start | bytes 98312 | tf_op jit(solution)/shard_map/ppermute | solution.py:582
  38.5 2.5 %copy-start.4 = (f32[8,3,512]{2,0,1:T(8,128)S(1)}, f32[8,3,512]{2,0,1:T(8,128)}, u32[]{:S(2)}) copy-start(f32[8,3,512]{2,0,1:T(8,128)} %param.21) | copy-start | bytes 147460

commit v4 on v3

--- a/solution.py
+++ b/solution.py
@@ -283,41 +283,50 @@
         out[t] = fold(sums)
 
 
-def lookup_kernel(table, tags, other_tags, out, far):
+def answer(table, tag, out, own):
     q = lax.axis_index("sec") & 1
     last = iota((8, L), 0) == 7
     total = table[pl.ds(25, 1), :]
     for p in range(1, CHIPS):
         total = total + table[pl.ds(p * ROWS + 25, 1), :]
     total = jnp.broadcast_to(total, (8, L))
-    for other, (tag, to) in enumerate(((tags, out), (other_tags, far))):
-        for h in range(2):
-            span = pl.ds(h * L, L)
-            own = jnp.broadcast_to(tag[pl.ds(0, 1), span], (8, L)).astype(jnp.int32)
-            lane = jnp.broadcast_to(tag[pl.ds(1, 1), span], (8, L)).astype(jnp.int32)
-            key = jnp.where((own & 1) == q, own >> 1, -1)
-            found = [jnp.zeros((8, L), F32) for _ in range(3)]
-            for p in range(CHIPS):
-                hit = key == p
-                for k in range(3):
-                    values = table[pl.ds(p * ROWS + k * NT, 8), :]
-                    found[k] = jnp.where(hit, lanes_of(values, lane), found[k])
+    for h in range(2):
+        span = pl.ds(h * L, L)
+        owner = jnp.broadcast_to(tag[pl.ds(0, 1), span], (8, L)).astype(jnp.int32)
+        lane = jnp.broadcast_to(tag[pl.ds(1, 1), span], (8, L)).astype(jnp.int32)
+        key = jnp.where((owner & 1) == q, owner >> 1, -1)
+        found = [jnp.zeros((8, L), F32) for _ in range(3)]
+        for p in range(CHIPS):
+            hit = key == p
             for k in range(3):
-                extra = 0.0 if other else jnp.broadcast_to(tag[pl.ds(2 + k, 1), span], (8, L))
-                to[pl.ds(h * 32 + k * 8, 8), :] = jnp.where(last, extra, found[k])
-            to[pl.ds(h * 32 + 24, 8), :] = total
-    for p in range(CHIPS):
-        far[pl.ds(64 + p * 8, 8), :] = table[pl.ds(p * ROWS + 19, 8), :]
-
-
-def node_sums(table, stride, base, dense):
+                values = table[pl.ds(p * ROWS + k * NT, 8), :]
+                found[k] = jnp.where(hit, lanes_of(values, lane), found[k])
+        for k in range(3):
+            extra = jnp.broadcast_to(tag[pl.ds(2 + k, 1), span], (8, L)) if own else 0.0
+            out[pl.ds(h * 32 + k * 8, 8), :] = jnp.where(last, extra, found[k])
+        out[pl.ds(h * 32 + 24, 8), :] = total
+
+
+def near_kernel(table, tags, out):
+    answer(table, tags, out, True)
+
+
+def far_kernel(table, other_tags, out):
+    answer(table, other_tags, out, False)
     q = lax.axis_index("sec") & 1
+    block = (iota((8, L), 1) >> 4) & 1
+    for p in range(CHIPS // 2):
+        first = table[pl.ds(2 * p * ROWS + 19, 8), :]
+        second = table[pl.ds((2 * p + 1) * ROWS + 19, 8), :]
+        first = jnp.where(q == 0, pltpu.roll(first, L - 16, 1), first)
+        second = jnp.where(q == 0, second, pltpu.roll(second, 16, 1))
+        out[pl.ds(64 + p * 8, 8), :] = jnp.where(block == 0, first, second)
+
+
+def node_sums(source, dense):
     block = iota((8, L), 1) >> 4
     for c in range(4):
-        shifted = []
-        for i in range(8):
-            values = table[pl.ds((c * 8 + i) * stride + base, 8), :]
-            shifted.append(jnp.where(q == 1, pltpu.roll(values, L - 16, 1), values))
+        shifted = [source(c * 8 + i) for i in range(8)]
         for g in range(4):
             packed = None
             for i in range(8):
@@ -332,11 +341,21 @@
 
 
 def own_loads_kernel(table, out, dense):
-    out[...] = node_sums(table, ROWS, 19, dense)
+    q = lax.axis_index("sec") & 1
+
+    def source(p):
+        values = table[pl.ds(p * ROWS + 19, 8), :]
+        return jnp.where(q == 1, pltpu.roll(values, L - 16, 1), values)
+
+    out[...] = node_sums(source, dense)
 
 
 def loads_kernel(other, sums, part, out, dense):
-    loads = node_sums(other, 8, 64, dense) + sums[...]
+    def source(p):
+        values = other[pl.ds(64 + p // 2 * 8, 8), :]
+        return pltpu.roll(values, L - 16, 1) if p % 2 else values
+
+    loads = node_sums(source, dense) + sums[...]
     for k, t, size, row in RUNS:
         out[k, pl.ds(t, size), :] = part[k, pl.ds(t, size), :] - loads[row : row + size]
 
@@ -568,15 +587,13 @@
         freq_delta,
     )
     mine, flux, far_edge = lax.optimization_barrier((mine, flux, far_edge))
-    near, far = kernel(lookup_kernel, "lookup", [VM] * 3, [(64, L), (320, L)])(
-        mine, tags, other_tags
-    )
+    (far,) = kernel(far_kernel, "far", [VM] * 2, [(192, L)])(mine, other_tags)
     back = lax.ppermute(far, "sec", swap)
+    (near,) = kernel(near_kernel, "near", [VM] * 2, [(64, L)])(mine, tags)
     (sums,) = kernel(
         own_loads_kernel, "own_loads", [VM], [(32, L)], scratch=[pltpu.VMEM((32, 512), F32)]
     )(mine)
-    (edge,) = kernel(edge_kernel, "edge", [VM] * 3, [(NT, NV, L)])(far_edge, jac, tags)
-    back, sums, edge = lax.optimization_barrier((back, sums, edge))
+    back, near, sums = lax.optimization_barrier((back, near, sums))
     disp = near + back[:64]
     d2, d3, d1 = (
         lax.ppermute(disp, "cell", [(i, i ^ k) for i in range(columns)]) for k in (2, 3, 1)
@@ -592,7 +609,8 @@
     moved, cols = kernel(own_kernel, "own", [VM] * 3, [(512, 48), (512, 32)])(
         disp, kept, bases[0]
     )
-    struct_out, moved, d2 = lax.optimization_barrier((struct_out, moved, d2))
+    (edge,) = kernel(edge_kernel, "edge", [VM] * 3, [(NT, NV, L)])(far_edge, jac, tags)
+    struct_out, moved, edge, d2 = lax.optimization_barrier((struct_out, moved, edge, d2))
     (moved,) = kernel(
         block_kernel,
         "block",

time: 42.5 us -> 42.2 us (level)
  transfers between devices with their start and end apart: 9 -> 9, of which waited for: 4 -> 4; matrix products, arithmetic and copies ran while one was open for 0% -> 0% of each run, Pallas kernels for 9% -> 10%
where the time goes in v4:
time: 42.2 us; the launch traced here: 41.9 us
  starting transfers between devices  27.3 us (65%)
  Pallas kernels  8.16 us (19%)
  waiting for transfers between devices  4.34 us (10%)
  between operations  2.07 us (5%)
    all_to_all x1, starting transfers between devices, on_device(): lax.all_to_all(message.reshape(CHIPS, 1, ROWS * L), 'sec', 0, 0, axis_ind...  12 us
    ppermute x1, starting transfers between devices, on_device(): far_edge = lax.ppermute(far_side, ('sec', 'cell'), pairs[1])  3.99 us
    ppermute x3, starting transfers between devices, on_device(): lax.ppermute(disp, 'cell', [(i, i ^ k) for i in range(columns)])  3.69 us
    ppermute x1, starting transfers between devices, on_device(): back = lax.ppermute(far, 'sec', swap)  3.14 us
    pallas_call x1, Pallas kernels, on_device(): kernel(prep_kernel, 'prep', [HBM] * 11, [(CHIPS * ROWS, L), (56, 256)], o...  2.63 us
    ppermute x1, starting transfers between devices, on_device(): lax.ppermute(centres, 'cell', [(i, i ^ 3) for i in range(columns)])  2.09 us
    pallas_call x1, Pallas kernels, on_device(): kernel(window_kernel, 'window', [VM] * 9, [(NT, NV, 512), (3, NT, L), (32...  2.01 us
    ppermute x3, waiting for transfers between devices, on_device(): lax.ppermute(disp, 'cell', [(i, i ^ k) for i in range(columns)])  1.74 us
  transfers between devices with their start and end apart: 9, of which 4 were waited for; matrix products, arithmetic and copies ran while one was open for 0% of the time, Pallas kernels for 10%

profile of v4, /device:TPU:1, one launch (start us, length us, event | category | flops | bytes accessed | tf_op | source)
XLA Modules:
  0.0 41.9 jit_solution(13756468459375232380)
XLA Ops:
  0.6 2.6 %prep.1 = (f32[864,128]{1,0:T(8,128)}, f32[56,256]{1,0:T(8,128)S(1)}) custom-call(f32[7,8,512]{2,1,0:T(8,128)} %fluid.3, f32[7,8,512]{2,1,0:T(8,128)} %refs_1_.1, s32[1,256]{1,0:T(1,128)} %bitcast.19, s32[1,256]{1,0:T(1,128)} %bitcast.20, s32[1,256]{1,0:T(1,128)} %bitcast.21, f32[3,8,256]{2,1,0:T(8,128)} %refs_5_.1, f32[3,7,128]{2,1,0:T(8,128)} %bitcast.18, ...), custom_call_target="tpu_custom_call" | custom-call | flops 1000 | bytes 100000 | tf_op jit(solution)/shard_map/prep/pallas_call | solution.py:510
  3.3 0.0 copy-start.1
  3.3 0.0 copy-start
  3.3 12.0 %all-to-all-start = ((f32[32,1,3456]{2,1,0:T(1,128)}), f32[32,1,3456]{2,1,0:T(1,128)S(1)}, u32[]{:S(2)}, u32[]{:S(2)}) async-start(f32[32,1,3456]{2,1,0:T(1,128)} %bitcast.4), calls=%async_computation | async-start | bytes 884736 | tf_op jit(solution)/shard_map/all_to_all | solution.py:553
  15.3 0.0 copy-start.3
  15.3 1.0 %collective-permute-start.3 = (f32[56,256]{1,0:T(8,128)S(1)}, f32[56,256]{1,0:T(8,128)S(1)}, u32[]{:S(2)}, u32[]{:S(2)}) collective-permute-start(f32[56,256]{1,0:T(8,128)S(1)} %get-tuple-element.30.tags), channel_id=1, source_target_pairs={{0,4},{4,0},{8,12},{12,8},{16,20},{20,16},{24,28},{28,24},{32,36},... | collective-permute-start | bytes 172040 | tf_op jit(solution)/shard_map/ppermute | solution.py:557
  16.4 1.4 %collective-permute-start = (f32[72,128]{1,0:T(8,128)S(1)}, f32[72,128]{1,0:T(8,128)S(1)}, u32[]{:S(2)}, u32[]{:S(2)}) collective-permute-start(f32[72,128]{1,0:T(8,128)S(1)} %get-tuple-element.31), channel_id=1, source_target_pairs={{0,1},{1,0},{2,3},{3,2},{4,5},{5,4},{6,7},{7,6},{8,9},{9,8},{10,11... | collective-permute-start | bytes 110600 | tf_op jit(solution)/shard_map/ppermute | solution.py:563
  17.8 4.0 %collective-permute-start.2 = (f32[7,8,128]{2,1,0:T(8,128)S(1)}, f32[7,8,128]{2,1,0:T(8,128)S(1)}, u32[]{:S(2)}, u32[]{:S(2)}) collective-permute-start(f32[7,8,128]{2,1,0:T(8,128)S(1)} %get-tuple-element.34), channel_id=1, source_target_pairs={{1,2},{2,1},{3,4},{4,3},{5,6},{6,5},{7,8},{8,7},{9,10},{10,9},{11,... | collective-permute-start | bytes 86024 | tf_op jit(solution)/shard_map/ppermute | solution.py:564
  21.8 2.1 %collective-permute-start.1 = (f32[16,128]{1,0:T(8,128)S(1)}, f32[16,128]{1,0:T(8,128)S(1)}, u32[]{:S(2)}, u32[]{:S(2)}) collective-permute-start(f32[16,128]{1,0:T(8,128)S(1)} %get-tuple-element.32), channel_id=1, source_target_pairs={{0,3},{1,2},{2,1},{3,0},{4,7},{5,6},{6,5},{7,4},{8,11},{9,10},{10,... | collective-permute-start | bytes 24584 | tf_op jit(solution)/shard_map/ppermute | solution.py:562
  25.2 0.7 %collective-permute-done.1.centres3 = f32[16,128]{1,0:T(8,128)S(1)} collective-permute-done((f32[16,128]{1,0:T(8,128)S(1)}, f32[16,128]{1,0:T(8,128)S(1)}, u32[]{:S(2)}, u32[]{:S(2)}) %collective-permute-start.1) | collective-permute-done | bytes 8224 | tf_op jit(solution)/shard_map/ppermute | solution.py:562
  25.9 0.0 collective-permute-done.near
  25.9 2.0 %window.1 = (f32[7,8,512]{2,1,0:T(8,128)S(1)}, f32[3,7,128]{2,1,0:T(8,128)S(1)}, f32[32,512]{1,0:T(8,128)S(1)}, bf16[512,512]{1,0:T(8,128)(2,1)S(1)}, bf16[512,5...) custom-call(f32[7,8,512]{2,1,0:T(8,128)S(1)} %copy-done.1, f32[72,128]{1,0:T(8,128)S(1)} %collective-permute-done.near, ...), custom_call_target="tpu_custom_call" | custom-call | flops 1000 | bytes 4000000 | tf_op jit(solution)/shard_map/window/pallas_call | solution.py:565
  27.9 0.0 collective-permute-done.2.far
  27.9 1.6 %all-to-all-done = f32[32,1,3456]{2,1,0:T(1,128)S(1)} async-done(((f32[32,1,3456]{2,1,0:T(1,128)}), f32[32,1,3456]{2,1,0:T(1,128)S(1)}, u32[]{:S(2)}, u32[]{:S(2)}) %all-to-all-start) | async-done | bytes 442400 | tf_op jit(solution)/shard_map/all_to_all | solution.py:553
  29.5 0.0 collective-permute-done.3.other_tags
  29.5 0.3 far.1
  29.8 3.1 %collective-permute-start.4 = (f32[192,128]{1,0:T(8,128)S(1)}, f32[192,128]{1,0:T(8,128)S(1)}, u32[]{:S(2)}, u32[]{:S(2)}) collective-permute-start(f32[192,128]{1,0:T(8,128)S(1)} %far.1), channel_id=1, source_target_pairs={{0,4},{4,0},{8,12},{12,8},{16,20},{20,16},{24,28},{28,24},{32,36},... | collective-permute-start | bytes 294920 | tf_op jit(solution)/shard_map/ppermute | solution.py:591
  33.0 0.3 near.1
  33.2 0.4 own_loads.1.sums
  33.6 0.3 collective-permute-done.4.other
  33.9 2.9 %collective-permute-start.6 = (f32[64,128]{1,0:T(8,128)S(1)}, f32[64,128]{1,0:T(8,128)S(1)}, u32[]{:S(2)}, u32[]{:S(2)}) collective-permute-start(f32[64,128]{1,0:T(8,128)S(1)} %slice_add_fusion.d0), channel_id=1, source_target_pairs={{0,2},{1,3},{2,0},{3,1},{4,6},{5,7},{6,4},{7,5},{8,10},{9,11},{10,... | collective-permute-start | bytes 98312 | tf_op jit(solution)/shard_map/ppermute | solution.py:599
  36.8 0.8 %collective-permute-start.7 = (f32[64,128]{1,0:T(8,128)S(1)}, f32[64,128]{1,0:T(8,128)S(1)}, u32[]{:S(2)}, u32[]{:S(2)}) collective-permute-start(f32[64,128]{1,0:T(8,128)S(1)} %slice_add_fusion.d0), channel_id=1, source_target_pairs={{0,3},{1,2},{2,1},{3,0},{4,7},{5,6},{6,5},{7,4},{8,11},{9,10},{10,... | collective-permute-start | bytes 98312 | tf_op jit(solution)/shard_map/ppermute | solution.py:599
  37.6 0.0 collective-permute-start.5
  37.6 0.2 edge.1
  37.8 0.4 loads.1.struct
  38.2 0.3 own.1
  38.5 0.0 collective-permute-done.6.ref.d2
  38.5 0.0 copy-start.4
  38.5 0.5 %block.1.moved = f32[512,48]{1,0:T(8,128)S(1)} custom-call(f32[64,128]{1,0:T(8,128)S(1)} %collective-permute-done.6.ref.d2, f32[512,32]{1,0:T(8,128)S(1)} %get-tuple-element.47.cols, f32[512,48]{1,0:T(8,128)S(1)} %get-tuple-element.48.moved), custom_call_target="tpu_custom_call" | custom-call | flops 1000 | bytes 1000000 | tf_op jit(solution)/shard_map/block/pallas_call | solution.py:614
  39.1 1.7 %collective-permute-done.7.d3 = f32[64,128]{1,0:T(8,128)S(1)} collective-permute-done((f32[64,128]{1,0:T(8,128)S(1)}, f32[64,128]{1,0:T(8,128)S(1)}, u32[]{:S(2)}, u32[]{:S(2)}) %collective-permute-start.7) | collective-permute-done | bytes 32800 | tf_op jit(solution)/shard_map/ppermute | solution.py:599
  40.8 0.0 collective-permute-done.5.d1
  40.8 1.1 %final.1 = (f32[7,8,512]{2,1,0:T(8,128)}, f32[3,7,128]{2,1,0:T(8,128)}, f32[1,1]{1,0:T(1,128)}) custom-call(f32[64,128]{1,0:T(8,128)S(1)} %slice_add_fusion.d0, f32[64,128]{1,0:T(8,128)S(1)} %collective-permute-done.5.d1, f32[64,128]{1,0:T(8,128)S(1)} %collective-permute-done.6.ref.d2, f32[64,128]{1,0:T(8,128)S(1)} %collective-permute-done.7.d3, ...), custom_call_target="tpu_custom_call" | custom-call | flops 1000 | bytes 100000 | tf_op jit(solution)/shard_map/final/pallas_call | solution.py:626
  (8 shorter events, 0.0 us)
Async XLA Ops:
  0.6 25.2 %copy-start.2 = (f32[3,128,3,128]{3,1,2,0:T(8,128)S(1)}, f32[3,128,3,128]{3,1,2,0:T(8,128)}, u32[]{:S(2)}) copy-start(f32[3,128,3,128]{3,1,2,0:T(8,128)} %param.29) | copy-start | bytes 1769476
  3.3 13.1 %copy-start.1 = (f32[7,8,512]{2,1,0:T(8,128)S(1)}, f32[7,8,512]{2,1,0:T(8,128)}, u32[]{:S(2)}) copy-start(f32[7,8,512]{2,1,0:T(8,128)} %fluid.3) | copy-start | bytes 344068
  3.3 22.6 %copy-start = (bf16[7,8,8,512]{3,2,1,0:T(8,128)(2,1)S(1)}, bf16[7,8,8,512]{3,2,1,0:T(8,128)(2,1)}, u32[]{:S(2)}) copy-start(bf16[7,8,8,512]{3,2,1,0:T(8,128)(2,1)} %param.18) | copy-start | bytes 1376260
  3.3 26.2 %all-to-all-start = ((f32[32,1,3456]{2,1,0:T(1,128)}), f32[32,1,3456]{2,1,0:T(1,128)S(1)}, u32[]{:S(2)}, u32[]{:S(2)}) async-start(f32[32,1,3456]{2,1,0:T(1,128)} %bitcast.4), calls=%async_computation | async-start | bytes 884736 | tf_op jit(solution)/shard_map/all_to_all | solution.py:553
  15.3 10.6 %copy-start.3 = (f32[7,8,512]{2,1,0:T(8,128)S(1)}, f32[7,8,512]{2,1,0:T(8,128)}, u32[]{:S(2)}) copy-start(f32[7,8,512]{2,1,0:T(8,128)} %freq.1) | copy-start | bytes 344068
  15.3 14.2 %collective-permute-start.3 = (f32[56,256]{1,0:T(8,128)S(1)}, f32[56,256]{1,0:T(8,128)S(1)}, u32[]{:S(2)}, u32[]{:S(2)}) collective-permute-start(f32[56,256]{1,0:T(8,128)S(1)} %get-tuple-element.30.tags), channel_id=1, source_target_pairs={{0,4},{4,0},{8,12},{12,8},{16,20},{20,16},{24,28},{28,24},{32,36},... | collective-permute-start | bytes 172040 | tf_op jit(solution)/shard_map/ppermute | solution.py:557
  16.4 9.5 %collective-permute-start = (f32[72,128]{1,0:T(8,128)S(1)}, f32[72,128]{1,0:T(8,128)S(1)}, u32[]{:S(2)}, u32[]{:S(2)}) collective-permute-start(f32[72,128]{1,0:T(8,128)S(1)} %get-tuple-element.31), channel_id=1, source_target_pairs={{0,1},{1,0},{2,3},{3,2},{4,5},{5,4},{6,7},{7,6},{8,9},{9,8},{10,11... | collective-permute-start | bytes 110600 | tf_op jit(solution)/shard_map/ppermute | solution.py:563
  17.8 10.1 %collective-permute-start.2 = (f32[7,8,128]{2,1,0:T(8,128)S(1)}, f32[7,8,128]{2,1,0:T(8,128)S(1)}, u32[]{:S(2)}, u32[]{:S(2)}) collective-permute-start(f32[7,8,128]{2,1,0:T(8,128)S(1)} %get-tuple-element.34), channel_id=1, source_target_pairs={{1,2},{2,1},{3,4},{4,3},{5,6},{6,5},{7,8},{8,7},{9,10},{10,9},{11,... | collective-permute-start | bytes 86024 | tf_op jit(solution)/shard_map/ppermute | solution.py:564
  21.8 4.1 %collective-permute-start.1 = (f32[16,128]{1,0:T(8,128)S(1)}, f32[16,128]{1,0:T(8,128)S(1)}, u32[]{:S(2)}, u32[]{:S(2)}) collective-permute-start(f32[16,128]{1,0:T(8,128)S(1)} %get-tuple-element.32), channel_id=1, source_target_pairs={{0,3},{1,2},{2,1},{3,0},{4,7},{5,6},{6,5},{7,4},{8,11},{9,10},{10,... | collective-permute-start | bytes 24584 | tf_op jit(solution)/shard_map/ppermute | solution.py:562
  29.8 4.1 %collective-permute-start.4 = (f32[192,128]{1,0:T(8,128)S(1)}, f32[192,128]{1,0:T(8,128)S(1)}, u32[]{:S(2)}, u32[]{:S(2)}) collective-permute-start(f32[192,128]{1,0:T(8,128)S(1)} %far.1), channel_id=1, source_target_pairs={{0,4},{4,0},{8,12},{12,8},{16,20},{20,16},{24,28},{28,24},{32,36},... | collective-permute-start | bytes 294920 | tf_op jit(solution)/shard_map/ppermute | solution.py:591
  33.9 4.6 %collective-permute-start.6 = (f32[64,128]{1,0:T(8,128)S(1)}, f32[64,128]{1,0:T(8,128)S(1)}, u32[]{:S(2)}, u32[]{:S(2)}) collective-permute-start(f32[64,128]{1,0:T(8,128)S(1)} %slice_add_fusion.d0), channel_id=1, source_target_pairs={{0,2},{1,3},{2,0},{3,1},{4,6},{5,7},{6,4},{7,5},{8,10},{9,11},{10,... | collective-permute-start | bytes 98312 | tf_op jit(solution)/shard_map/ppermute | solution.py:599
  36.8 4.0 %collective-permute-start.7 = (f32[64,128]{1,0:T(8,128)S(1)}, f32[64,128]{1,0:T(8,128)S(1)}, u32[]{:S(2)}, u32[]{:S(2)}) collective-permute-start(f32[64,128]{1,0:T(8,128)S(1)} %slice_add_fusion.d0), channel_id=1, source_target_pairs={{0,3},{1,2},{2,1},{3,0},{4,7},{5,6},{6,5},{7,4},{8,11},{9,10},{10,... | collective-permute-start | bytes 98312 | tf_op jit(solution)/shard_map/ppermute | solution.py:599
  37.6 3.2 %collective-permute-start.5 = (f32[64,128]{1,0:T(8,128)S(1)}, f32[64,128]{1,0:T(8,128)S(1)}, u32[]{:S(2)}, u32[]{:S(2)}) collective-permute-start(f32[64,128]{1,0:T(8,128)S(1)} %slice_add_fusion.d0), channel_id=1, source_target_pairs={{0,1},{1,0},{2,3},{3,2},{4,5},{5,4},{6,7},{7,6},{8,9},{9,8},{10,11... | collective-permute-start | bytes 98312 | tf_op jit(solution)/shard_map/ppermute | solution.py:599
  38.5 2.3 %copy-start.4 = (f32[8,3,512]{2,0,1:T(8,128)S(1)}, f32[8,3,512]{2,0,1:T(8,128)}, u32[]{:S(2)}) copy-start(f32[8,3,512]{2,0,1:T(8,128)} %param.21) | copy-start | bytes 147460

commit v5 on v4

--- a/solution.py
+++ b/solution.py
@@ -423,13 +423,16 @@
     out[...] = moved[...] + moved_by(both, basis)
 
 
+def third_kernel(d3, basis, moved, out):
+    out[...] = moved[...] + moved_by(halves(d3), basis)
+
+
 def final_kernel(
     d0,
     d1,
     d2,
     d3,
     near_basis,
-    third_basis,
     moved,
     sens,
     flux,
@@ -442,7 +445,7 @@
     struct_out[...] = struct[...]
     even = (lax.axis_index("cell") & 1) == 0
     span = pl.ds(pl.multiple_of(jnp.where(even, 0, 3 * L), L), L)
-    total = moved[...] + moved_by(halves(d3), third_basis) + moved_by(halves(d1), near_basis)
+    total = moved[...] + moved_by(halves(d1), near_basis)
     turned = total.T
     motion = turned[0:24] + turned[24:48]
     for t in range(NT):
@@ -623,13 +626,14 @@
         ],
         size=10**6,
     )(d2, cols, moved)
+    (moved,) = kernel(third_kernel, "third", [VM] * 3, [(512, 48)])(d3, bases[2], moved)
     fluid_out, struct_out, phase_out = kernel(
         final_kernel,
         "final",
-        [VM] * 11,
+        [VM] * 10,
         [(NT, NV, 512), (3, NT, L), (1, 1)],
         outs=[VM, VM, SM],
-    )(disp, d1, d2, d3, bases[1], bases[2], moved, sens, flux, edge, struct_out)
+    )(disp, d1, d2, d3, bases[1], moved, sens, flux, edge, struct_out)
     return fluid_out, jnp.transpose(struct_out, (1, 0, 2)), phase_out.reshape(1)
 
 

time: 42.2 us -> 42.9 us (1.017)
  local copies, waits for them, and re-layouts: 0.03 us -> 0.54 us
    unnamed x10, local copies, waits for them, and re-layouts: 0.03 us -> 0.54 us
    pallas_call x1 -> x2, Pallas kernels: 1.14 us -> 1.27 us  [the longest x1 1 us: on_device(): kernel(final_kernel, 'final', [VM] * 10, [(NT, NV, 512), (3, NT, L), (1,...]
where the time goes in v5:
time: 42.9 us; the launch traced here: 42.6 us
  starting transfers between devices  27.3 us (64%)
  Pallas kernels  8.28 us (19%)
  waiting for transfers between devices  4.36 us (10%)
  between operations  2.08 us (5%)
  local copies, waits for them, and re-layouts  0.54 us (1%)
    all_to_all x1, starting transfers between devices, on_device(): lax.all_to_all(message.reshape(CHIPS, 1, ROWS * L), 'sec', 0, 0, axis_ind...  12 us
    ppermute x1, starting transfers between devices, on_device(): far_edge = lax.ppermute(far_side, ('sec', 'cell'), pairs[1])  3.99 us
    ppermute x3, starting transfers between devices, on_device(): lax.ppermute(disp, 'cell', [(i, i ^ k) for i in range(columns)])  3.69 us
    ppermute x1, starting transfers between devices, on_device(): back = lax.ppermute(far, 'sec', swap)  3.14 us
    pallas_call x1, Pallas kernels, on_device(): kernel(prep_kernel, 'prep', [HBM] * 11, [(CHIPS * ROWS, L), (56, 256)], o...  2.63 us
    ppermute x1, starting transfers between devices, on_device(): lax.ppermute(centres, 'cell', [(i, i ^ 3) for i in range(columns)])  2.09 us
    pallas_call x1, Pallas kernels, on_device(): kernel(window_kernel, 'window', [VM] * 9, [(NT, NV, 512), (3, NT, L), (32...  2.01 us
    ppermute x3, waiting for transfers between devices, on_device(): lax.ppermute(disp, 'cell', [(i, i ^ k) for i in range(columns)])  1.77 us
  transfers between devices with their start and end apart: 9, of which 4 were waited for; matrix products, arithmetic and copies ran while one was open for 0% of the time, Pallas kernels for 10%

profile of v5, /device:TPU:1, one launch (start us, length us, event | category | flops | bytes accessed | tf_op | source)
XLA Modules:
  0.0 42.6 jit_solution(4931999968565978621)
XLA Ops:
  0.6 2.6 %prep.1 = (f32[864,128]{1,0:T(8,128)}, f32[56,256]{1,0:T(8,128)S(1)}) custom-call(f32[7,8,512]{2,1,0:T(8,128)} %fluid.3, f32[7,8,512]{2,1,0:T(8,128)} %refs_1_.1, s32[1,256]{1,0:T(1,128)} %bitcast.19, s32[1,256]{1,0:T(1,128)} %bitcast.20, s32[1,256]{1,0:T(1,128)} %bitcast.21, f32[3,8,256]{2,1,0:T(8,128)} %refs_5_.1, f32[3,7,128]{2,1,0:T(8,128)} %bitcast.18, ...), custom_call_target="tpu_custom_call" | custom-call | flops 1000 | bytes 100000 | tf_op jit(solution)/shard_map/prep/pallas_call | solution.py:513
  3.3 0.0 copy-start.1
  3.3 0.0 copy-start
  3.3 12.0 %all-to-all-start = ((f32[32,1,3456]{2,1,0:T(1,128)}), f32[32,1,3456]{2,1,0:T(1,128)S(1)}, u32[]{:S(2)}, u32[]{:S(2)}) async-start(f32[32,1,3456]{2,1,0:T(1,128)} %bitcast.4), calls=%async_computation | async-start | bytes 884736 | tf_op jit(solution)/shard_map/all_to_all | solution.py:556
  15.3 0.0 copy-start.3
  15.3 1.0 %collective-permute-start.3 = (f32[56,256]{1,0:T(8,128)S(1)}, f32[56,256]{1,0:T(8,128)S(1)}, u32[]{:S(2)}, u32[]{:S(2)}) collective-permute-start(f32[56,256]{1,0:T(8,128)S(1)} %get-tuple-element.30.tags), channel_id=1, source_target_pairs={{0,4},{4,0},{8,12},{12,8},{16,20},{20,16},{24,28},{28,24},{32,36},... | collective-permute-start | bytes 172040 | tf_op jit(solution)/shard_map/ppermute | solution.py:560
  16.4 1.4 %collective-permute-start = (f32[72,128]{1,0:T(8,128)S(1)}, f32[72,128]{1,0:T(8,128)S(1)}, u32[]{:S(2)}, u32[]{:S(2)}) collective-permute-start(f32[72,128]{1,0:T(8,128)S(1)} %get-tuple-element.31), channel_id=1, source_target_pairs={{0,1},{1,0},{2,3},{3,2},{4,5},{5,4},{6,7},{7,6},{8,9},{9,8},{10,11... | collective-permute-start | bytes 110600 | tf_op jit(solution)/shard_map/ppermute | solution.py:566
  17.8 4.0 %collective-permute-start.2 = (f32[7,8,128]{2,1,0:T(8,128)S(1)}, f32[7,8,128]{2,1,0:T(8,128)S(1)}, u32[]{:S(2)}, u32[]{:S(2)}) collective-permute-start(f32[7,8,128]{2,1,0:T(8,128)S(1)} %get-tuple-element.34), channel_id=1, source_target_pairs={{1,2},{2,1},{3,4},{4,3},{5,6},{6,5},{7,8},{8,7},{9,10},{10,9},{11,... | collective-permute-start | bytes 86024 | tf_op jit(solution)/shard_map/ppermute | solution.py:567
  21.8 2.1 %collective-permute-start.1 = (f32[16,128]{1,0:T(8,128)S(1)}, f32[16,128]{1,0:T(8,128)S(1)}, u32[]{:S(2)}, u32[]{:S(2)}) collective-permute-start(f32[16,128]{1,0:T(8,128)S(1)} %get-tuple-element.32), channel_id=1, source_target_pairs={{0,3},{1,2},{2,1},{3,0},{4,7},{5,6},{6,5},{7,4},{8,11},{9,10},{10,... | collective-permute-start | bytes 24584 | tf_op jit(solution)/shard_map/ppermute | solution.py:565
  25.2 0.7 %collective-permute-done.1.centres3 = f32[16,128]{1,0:T(8,128)S(1)} collective-permute-done((f32[16,128]{1,0:T(8,128)S(1)}, f32[16,128]{1,0:T(8,128)S(1)}, u32[]{:S(2)}, u32[]{:S(2)}) %collective-permute-start.1) | collective-permute-done | bytes 8224 | tf_op jit(solution)/shard_map/ppermute | solution.py:565
  25.9 0.0 collective-permute-done.near
  25.9 2.0 %window.1 = (f32[7,8,512]{2,1,0:T(8,128)S(1)}, f32[3,7,128]{2,1,0:T(8,128)S(1)}, f32[32,512]{1,0:T(8,128)S(1)}, bf16[512,512]{1,0:T(8,128)(2,1)S(1)}, bf16[512,5...) custom-call(f32[7,8,512]{2,1,0:T(8,128)S(1)} %copy-done.1, f32[72,128]{1,0:T(8,128)S(1)} %collective-permute-done.near, ...), custom_call_target="tpu_custom_call" | custom-call | flops 1000 | bytes 4000000 | tf_op jit(solution)/shard_map/window/pallas_call | solution.py:568
  27.9 0.0 collective-permute-done.2.far
  27.9 1.6 %all-to-all-done = f32[32,1,3456]{2,1,0:T(1,128)S(1)} async-done(((f32[32,1,3456]{2,1,0:T(1,128)}), f32[32,1,3456]{2,1,0:T(1,128)S(1)}, u32[]{:S(2)}, u32[]{:S(2)}) %all-to-all-start) | async-done | bytes 442400 | tf_op jit(solution)/shard_map/all_to_all | solution.py:556
  29.5 0.0 collective-permute-done.3.other_tags
  29.5 0.3 far.1
  29.8 3.1 %collective-permute-start.4 = (f32[192,128]{1,0:T(8,128)S(1)}, f32[192,128]{1,0:T(8,128)S(1)}, u32[]{:S(2)}, u32[]{:S(2)}) collective-permute-start(f32[192,128]{1,0:T(8,128)S(1)} %far.1), channel_id=1, source_target_pairs={{0,4},{4,0},{8,12},{12,8},{16,20},{20,16},{24,28},{28,24},{32,36},... | collective-permute-start | bytes 294920 | tf_op jit(solution)/shard_map/ppermute | solution.py:594
  33.0 0.3 near.1
  33.2 0.4 own_loads.1.sums
  33.6 0.3 collective-permute-done.4.other
  33.9 2.9 %collective-permute-start.6 = (f32[64,128]{1,0:T(8,128)S(1)}, f32[64,128]{1,0:T(8,128)S(1)}, u32[]{:S(2)}, u32[]{:S(2)}) collective-permute-start(f32[64,128]{1,0:T(8,128)S(1)} %slice_add_fusion.d0), channel_id=1, source_target_pairs={{0,2},{1,3},{2,0},{3,1},{4,6},{5,7},{6,4},{7,5},{8,10},{9,11},{10,... | collective-permute-start | bytes 98312 | tf_op jit(solution)/shard_map/ppermute | solution.py:602
  36.8 0.8 %collective-permute-start.7 = (f32[64,128]{1,0:T(8,128)S(1)}, f32[64,128]{1,0:T(8,128)S(1)}, u32[]{:S(2)}, u32[]{:S(2)}) collective-permute-start(f32[64,128]{1,0:T(8,128)S(1)} %slice_add_fusion.d0), channel_id=1, source_target_pairs={{0,3},{1,2},{2,1},{3,0},{4,7},{5,6},{6,5},{7,4},{8,11},{9,10},{10,... | collective-permute-start | bytes 98312 | tf_op jit(solution)/shard_map/ppermute | solution.py:602
  37.6 0.0 collective-permute-start.5
  37.6 0.2 edge.1
  37.8 0.4 loads.1.struct
  38.2 0.3 own.1
  38.5 0.0 collective-permute-done.6.ref.d2
  38.5 0.5 %block.1.moved = f32[512,48]{1,0:T(8,128)S(1)} custom-call(f32[64,128]{1,0:T(8,128)S(1)} %collective-permute-done.6.ref.d2, f32[512,32]{1,0:T(8,128)S(1)} %get-tuple-element.47.cols, f32[512,48]{1,0:T(8,128)S(1)} %get-tuple-element.48.moved), custom_call_target="tpu_custom_call" | custom-call | flops 1000 | bytes 1000000 | tf_op jit(solution)/shard_map/block/pallas_call | solution.py:617
  39.0 1.8 %collective-permute-done.7.d3 = f32[64,128]{1,0:T(8,128)S(1)} collective-permute-done((f32[64,128]{1,0:T(8,128)S(1)}, f32[64,128]{1,0:T(8,128)S(1)}, u32[]{:S(2)}, u32[]{:S(2)}) %collective-permute-start.7) | collective-permute-done | bytes 32800 | tf_op jit(solution)/shard_map/ppermute | solution.py:602
  40.8 0.3 third.1.moved
  41.1 0.5 %copy-done.4 = f32[8,3,512]{2,0,1:T(8,128)S(1)} copy-done((f32[8,3,512]{2,0,1:T(8,128)S(1)}, f32[8,3,512]{2,0,1:T(8,128)}, u32[]{:S(2)}) %copy-start.4) | copy-done | bytes 49176
  41.6 1.0 %final.1 = (f32[7,8,512]{2,1,0:T(8,128)}, f32[3,7,128]{2,1,0:T(8,128)}, f32[1,1]{1,0:T(1,128)}) custom-call(f32[64,128]{1,0:T(8,128)S(1)} %slice_add_fusion.d0, f32[64,128]{1,0:T(8,128)S(1)} %collective-permute-done.5.d1, f32[64,128]{1,0:T(8,128)S(1)} %collective-permute-done.6.ref.d2, f32[64,128]{1,0:T(8,128)S(1)} %collective-permute-done.7.d3, ...), custom_call_target="tpu_custom_call" | custom-call | flops 1000 | bytes 100000 | tf_op jit(solution)/shard_map/final/pallas_call | solution.py:630
  (9 shorter events, 0.0 us)
Async XLA Ops:
  0.6 25.2 %copy-start.2 = (f32[3,128,3,128]{3,1,2,0:T(8,128)S(1)}, f32[3,128,3,128]{3,1,2,0:T(8,128)}, u32[]{:S(2)}) copy-start(f32[3,128,3,128]{3,1,2,0:T(8,128)} %param.29) | copy-start | bytes 1769476
  3.3 13.1 %copy-start.1 = (f32[7,8,512]{2,1,0:T(8,128)S(1)}, f32[7,8,512]{2,1,0:T(8,128)}, u32[]{:S(2)}) copy-start(f32[7,8,512]{2,1,0:T(8,128)} %fluid.3) | copy-start | bytes 344068
  3.3 22.6 %copy-start = (bf16[7,8,8,512]{3,2,1,0:T(8,128)(2,1)S(1)}, bf16[7,8,8,512]{3,2,1,0:T(8,128)(2,1)}, u32[]{:S(2)}) copy-start(bf16[7,8,8,512]{3,2,1,0:T(8,128)(2,1)} %param.18) | copy-start | bytes 1376260
  3.3 26.2 %all-to-all-start = ((f32[32,1,3456]{2,1,0:T(1,128)}), f32[32,1,3456]{2,1,0:T(1,128)S(1)}, u32[]{:S(2)}, u32[]{:S(2)}) async-start(f32[32,1,3456]{2,1,0:T(1,128)} %bitcast.4), calls=%async_computation | async-start | bytes 884736 | tf_op jit(solution)/shard_map/all_to_all | solution.py:556
  15.3 10.6 %copy-start.3 = (f32[7,8,512]{2,1,0:T(8,128)S(1)}, f32[7,8,512]{2,1,0:T(8,128)}, u32[]{:S(2)}) copy-start(f32[7,8,512]{2,1,0:T(8,128)} %freq.1) | copy-start | bytes 344068
  15.3 14.2 %collective-permute-start.3 = (f32[56,256]{1,0:T(8,128)S(1)}, f32[56,256]{1,0:T(8,128)S(1)}, u32[]{:S(2)}, u32[]{:S(2)}) collective-permute-start(f32[56,256]{1,0:T(8,128)S(1)} %get-tuple-element.30.tags), channel_id=1, source_target_pairs={{0,4},{4,0},{8,12},{12,8},{16,20},{20,16},{24,28},{28,24},{32,36},... | collective-permute-start | bytes 172040 | tf_op jit(solution)/shard_map/ppermute | solution.py:560
  16.4 9.5 %collective-permute-start = (f32[72,128]{1,0:T(8,128)S(1)}, f32[72,128]{1,0:T(8,128)S(1)}, u32[]{:S(2)}, u32[]{:S(2)}) collective-permute-start(f32[72,128]{1,0:T(8,128)S(1)} %get-tuple-element.31), channel_id=1, source_target_pairs={{0,1},{1,0},{2,3},{3,2},{4,5},{5,4},{6,7},{7,6},{8,9},{9,8},{10,11... | collective-permute-start | bytes 110600 | tf_op jit(solution)/shard_map/ppermute | solution.py:566
  17.8 10.1 %collective-permute-start.2 = (f32[7,8,128]{2,1,0:T(8,128)S(1)}, f32[7,8,128]{2,1,0:T(8,128)S(1)}, u32[]{:S(2)}, u32[]{:S(2)}) collective-permute-start(f32[7,8,128]{2,1,0:T(8,128)S(1)} %get-tuple-element.34), channel_id=1, source_target_pairs={{1,2},{2,1},{3,4},{4,3},{5,6},{6,5},{7,8},{8,7},{9,10},{10,9},{11,... | collective-permute-start | bytes 86024 | tf_op jit(solution)/shard_map/ppermute | solution.py:567
  21.8 4.1 %collective-permute-start.1 = (f32[16,128]{1,0:T(8,128)S(1)}, f32[16,128]{1,0:T(8,128)S(1)}, u32[]{:S(2)}, u32[]{:S(2)}) collective-permute-start(f32[16,128]{1,0:T(8,128)S(1)} %get-tuple-element.32), channel_id=1, source_target_pairs={{0,3},{1,2},{2,1},{3,0},{4,7},{5,6},{6,5},{7,4},{8,11},{9,10},{10,... | collective-permute-start | bytes 24584 | tf_op jit(solution)/shard_map/ppermute | solution.py:565
  29.8 4.1 %collective-permute-start.4 = (f32[192,128]{1,0:T(8,128)S(1)}, f32[192,128]{1,0:T(8,128)S(1)}, u32[]{:S(2)}, u32[]{:S(2)}) collective-permute-start(f32[192,128]{1,0:T(8,128)S(1)} %far.1), channel_id=1, source_target_pairs={{0,4},{4,0},{8,12},{12,8},{16,20},{20,16},{24,28},{28,24},{32,36},... | collective-permute-start | bytes 294920 | tf_op jit(solution)/shard_map/ppermute | solution.py:594
  33.9 4.6 %collective-permute-start.6 = (f32[64,128]{1,0:T(8,128)S(1)}, f32[64,128]{1,0:T(8,128)S(1)}, u32[]{:S(2)}, u32[]{:S(2)}) collective-permute-start(f32[64,128]{1,0:T(8,128)S(1)} %slice_add_fusion.d0), channel_id=1, source_target_pairs={{0,2},{1,3},{2,0},{3,1},{4,6},{5,7},{6,4},{7,5},{8,10},{9,11},{10,... | collective-permute-start | bytes 98312 | tf_op jit(solution)/shard_map/ppermute | solution.py:602
  36.8 4.0 %collective-permute-start.7 = (f32[64,128]{1,0:T(8,128)S(1)}, f32[64,128]{1,0:T(8,128)S(1)}, u32[]{:S(2)}, u32[]{:S(2)}) collective-permute-start(f32[64,128]{1,0:T(8,128)S(1)} %slice_add_fusion.d0), channel_id=1, source_target_pairs={{0,3},{1,2},{2,1},{3,0},{4,7},{5,6},{6,5},{7,4},{8,11},{9,10},{10,... | collective-permute-start | bytes 98312 | tf_op jit(solution)/shard_map/ppermute | solution.py:602
  37.6 3.5 %collective-permute-start.5 = (f32[64,128]{1,0:T(8,128)S(1)}, f32[64,128]{1,0:T(8,128)S(1)}, u32[]{:S(2)}, u32[]{:S(2)}) collective-permute-start(f32[64,128]{1,0:T(8,128)S(1)} %slice_add_fusion.d0), channel_id=1, source_target_pairs={{0,1},{1,0},{2,3},{3,2},{4,5},{5,4},{6,7},{7,6},{8,9},{9,8},{10,11... | collective-permute-start | bytes 98312 | tf_op jit(solution)/shard_map/ppermute | solution.py:602
  40.8 0.8 %copy-start.4 = (f32[8,3,512]{2,0,1:T(8,128)S(1)}, f32[8,3,512]{2,0,1:T(8,128)}, u32[]{:S(2)}) copy-start(f32[8,3,512]{2,0,1:T(8,128)} %param.21) | copy-start | bytes 147460
